TPU v7x, 512 devices: a whole 4x8x8 slice. The times are simulated.
512 devices in a mesh: group: 16 (over z, core), table: 32 (over y, x).
Axes of the slice: x: 4, y: 8, z: 8, core: 2. Of those that a mesh axis runs over, the one named last changes fastest.
Arguments:
- embedded: bfloat16 [65536, 4096], P(('group', 'table')), may hold values from -6 to 6
- ngram_ids: int32 [65536, 4], P(('group', 'table')), may hold values from 0 to 6143, as said below
- counts: int32 [65536], P(('group', 'table')), may hold values from 1 to 4
- slab: bfloat16 [6144, 4096], P('table'), may hold values from -6 to 6
- gain: bfloat16 [4096], replicated, may hold values from 0.099609375 to 1.8984375
- cotangent: bfloat16 [65536, 4096], P(('group', 'table')), may hold values from -6 to 6
Outputs:
- normed: bfloat16 [65536, 4096], P(('group', 'table'))
- grad_slab: float32 [6144, 4096], P('table', 'group')
Inputs may be any that keep to these rules, and one draw needn't show every extreme that they name: ngram_ids[t, k] = o * 192 + r names row r of table device o. Among the 512 slots of one device, a quarter of the table devices receive exactly 24 slots, half receive exactly 16 and a quarter exactly 8; which table devices receive most is the same for all devices of one group. Slots past a token's count carry ids as well.
All inputs are finite; a program needn't handle non-finite values.
Results may differ from a plain program's by a relative error of at most 0.0029.
Values may be sent and summed in bfloat16 or wider, within the bound.
No kernel may reach another device: no remote copies, remote signals or barrier semaphores. Data moves between devices by JAX's collectives and lax.ppermute only.
A program may use at most 64 MiB of HBM per device.

v0:
```python
import jax
import jax.numpy as jnp
from jax import lax
from jax.sharding import PartitionSpec as P


def per_device(embedded, ngram_ids, counts, slab, gain, cotangent):
    tok_rows, features = embedded.shape
    ngram = ngram_ids.shape[1]
    slab_rows = slab.shape[0]
    table_size = lax.axis_size("table")
    capacity = 3 * tok_rows * ngram // (2 * table_size)
    every_slot_index = table_size * capacity
    owner_index = ngram_ids // slab_rows
    local_row = ngram_ids % slab_rows
    owner_hot = (owner_index.reshape(-1)[:, None] == jnp.arange(table_size)[None, :]).astype(
        jnp.int32
    )
    position = jnp.sum((jnp.cumsum(owner_hot, axis=0) - 1) * owner_hot, axis=1).reshape(
        tok_rows, ngram
    )
    slot_index = owner_index * capacity + position
    request = (
        jnp.full((every_slot_index,), -1, jnp.int32)
        .at[slot_index.reshape(-1)]
        .set(local_row.reshape(-1))
    )
    request = request.reshape(table_size, capacity)
    live_slot = jnp.arange(ngram)[None, :] < counts[:, None]
    requested = lax.all_to_all(request, "table", split_axis=0, concat_axis=0, tiled=True)
    indicator_matrix = (requested[:, :, None] == jnp.arange(slab_rows)[None, None, :]).astype(
        jnp.bfloat16
    )
    lookup_result = jnp.einsum(
        "ozl,ln->ozn", indicator_matrix, slab, preferred_element_type=jnp.float32
    ).astype(jnp.bfloat16)
    returned = lax.all_to_all(lookup_result, "table", split_axis=0, concat_axis=0, tiled=True)
    select = jnp.any(
        (slot_index[:, :, None] == jnp.arange(every_slot_index)[None, None, :])
        & live_slot[:, :, None],
        axis=1,
    )
    select = select.astype(jnp.bfloat16)
    count_f = counts[:, None].astype(jnp.float32)
    pooled = (
        jnp.dot(
            select, returned.reshape(every_slot_index, features), preferred_element_type=jnp.float32
        )
        / count_f
    )
    hidden = embedded.astype(jnp.float32) + pooled
    gain_f = gain.astype(jnp.float32)
    inv_rms = lax.rsqrt(jnp.mean(hidden * hidden, axis=-1, keepdims=True) + 1e-05)
    normed = (hidden * inv_rms * gain_f).astype(jnp.bfloat16)
    grad_out = cotangent.astype(jnp.float32) * gain_f
    inner_term = jnp.mean(hidden * grad_out, axis=-1, keepdims=True)
    grad_hidden = inv_rms * grad_out - hidden * (inv_rms * inv_rms * inv_rms) * inner_term
    token_grad = (grad_hidden / count_f).astype(jnp.bfloat16)
    slot_grad = jnp.einsum(
        "tj,td->jd", select, token_grad, preferred_element_type=jnp.float32
    ).astype(jnp.bfloat16)
    arrived = lax.all_to_all(
        slot_grad.reshape(table_size, capacity, features),
        "table",
        split_axis=0,
        concat_axis=0,
        tiled=True,
    )
    served_hot = (requested.reshape(-1)[:, None] == jnp.arange(slab_rows)[None, :]).astype(
        jnp.bfloat16
    )
    partial_sum = jnp.einsum(
        "jr,jd->rd",
        served_hot,
        arrived.reshape(every_slot_index, features),
        preferred_element_type=jnp.float32,
    )
    row_grads = lax.psum_scatter(partial_sum, "group", scatter_dimension=1, tiled=True)
    return (normed, row_grads)


def solution(mesh):
    in_specs = (
        P(("group", "table"), None),
        P(("group", "table"), None),
        P(("group", "table")),
        P("table", None),
        P(),
        P(("group", "table"), None),
    )
    out_specs = (P(("group", "table"), None), P("table", "group"))
    return jax.shard_map(
        per_device, mesh=mesh, in_specs=in_specs, out_specs=out_specs, check_vma=False
    )
```

profile of v0, /device:TPU:1, one launch (start us, length us, event | category | flops | bytes accessed | tf_op | source)
XLA Modules:
  0.0 418.6 jit_solution(10782109267838444838)
XLA Ops:
  7.2 0.0 copy-start
  7.2 0.8 add_select_fusion
  8.0 0.1 copy.33
  8.1 0.1 eq.74
  8.2 0.1 eq.70
  8.3 0.1 copy.38
  8.4 0.1 reshape.131
  8.6 1.2 reduce-window.6
  9.7 0.2 slice_reduce_fusion
  10.0 0.1 fusion.13
  10.1 0.1 reshape.121
  10.2 0.1 copy.36
  10.3 0.1 copy.37
  10.4 0.1 reshape.122
  10.5 2.4 scatter_custom_fusion
  13.0 0.1 all_to_all.12
  13.1 18.9 %all_to_all.19 = s32[32,1,24]{2,1,0:T(1,128)S(1)} all-to-all(s32[32,1,24]{2,1,0:T(1,128)S(1)} %bitcast.31), channel_id=1, replica_groups=mesh['group'=16,'table'=32] {'table'}, dimensions={0} | all-to-all | bytes 6144 | tf_op jit(solution)/shard_map/all_to_all | solution.py:30
  32.0 0.0 copy-done
  32.0 4.5 %convolution_convert_fusion.1 = bf16[32,24,4096]{2,1,0:T(8,128)(2,1)} fusion(bf16[192,4096]{1,0:T(8,128)(2,1)S(1)} %copy-done, s32[32,24]{1,0:T(8,128)S(1)} %bitcast.30), kind=kOutput, calls=%fused_computation.2 | convolution fusion | flops 1211252736 | bytes 7867392 | tf_op jit(solution)/shard_map/ozl,ln->ozn/dot_general | solution.py:34
  36.5 0.0 copy-start.5
  36.5 0.0 copy-start.2
  36.5 0.0 copy-start.3
  36.5 5.0 %all-to-all-start.1 = ((bf16[32,24,4096]{2,1,0:T(8,128)(2,1)}), bf16[32,24,4096]{2,1,0:T(8,128)(2,1)}, u32[]{:S(2)}, u32[]{:S(2)}) async-start(bf16[32,24,4096]{2,1,0:T(8,128)(2,1)} %convolution_convert_fusion.1), calls=%async_computation.1 | async-start | bytes 12582912 | tf_op jit(solution)/shard_map/all_to_all | solution.py:37
  41.5 0.0 copy-done.5
  41.5 0.0 copy-done.2
  41.6 0.3 fusion.3
  41.9 135.5 %all-to-all-done.1 = bf16[32,24,4096]{2,1,0:T(8,128)(2,1)} async-done(((bf16[32,24,4096]{2,1,0:T(8,128)(2,1)}), bf16[32,24,4096]{2,1,0:T(8,128)(2,1)}, u32[]{:S(2)}, u32[]{:S(2)}) %all-to-all-start.1) | async-done | bytes 6291488 | tf_op jit(solution)/shard_map/all_to_all | solution.py:37
  177.4 0.0 copy-done.3
  177.4 0.0 copy-start.4
  177.4 4.9 %multiply_reduce_fusion = (f32[128]{0:T(128)S(1)}, f32[128]{0:T(128)S(1)}, f32[128,4096]{1,0:T(8,128)S(1)}) fusion(bf16[128,4096]{1,0:T(8,128)(2,1)} %param.11, f32[4096]{0:T(1024)S(1)} %convert_element_type.37, f32[128]{0:T(128)S(1)} %convert_element_type.36, pred[128,768]{1,0:T(8,128)(4,1)S(1)} %fusion.3, bf16[768,4096]{1,0:T(8,128)(2,1)} %bitcast.5, ...), kind=kOutput, calls=%fused_computation.6 | convolution fusion | flops 810024704 | bytes 10601984 | tf_op jit(solution)/shard_map/dot_general | solution.py:46
  182.3 0.0 copy-start.1
  182.3 0.0 copy-done.4
  182.3 4.7 %convolution_convert_fusion = bf16[768,4096]{1,0:T(8,128)(2,1)} fusion(pred[128,768]{1,0:T(8,128)(4,1)S(1)} %fusion.3, f32[128,4096]{1,0:T(8,128)S(1)} %get-tuple-element.8, bf16[128,4096]{1,0:T(8,128)(2,1)S(1)} %copy-done.4, f32[128]{0:T(128)S(1)} %get-tuple-element.9, f32[128]{0:T(128)S(1)} %get-tuple-element.6, f32[4096]{0:T(1024)S(1)} %convert_element_type.37, ...), kind=kOutput, calls=%fused_computation.1 | convolution fusion | flops 812646400 | bytes 9553920 | tf_op jit(solution)/shard_map/tj,td->jd/dot_general | solution.py:59
  187.0 0.0 copy-done.1
  187.0 10.4 %all-to-all-start.2 = ((bf16[32,24,4096]{2,1,0:T(8,128)(2,1)}), bf16[32,24,4096]{2,1,0:T(8,128)(2,1)}, u32[]{:S(2)}, u32[]{:S(2)}) async-start(bf16[32,24,4096]{2,1,0:T(8,128)(2,1)} %bitcast.29), calls=%async_computation.2 | async-start | bytes 12582912 | tf_op jit(solution)/shard_map/all_to_all | solution.py:62
  197.4 0.0 reduce-scatter.2.cloned.1.call-start
  197.5 0.5 broadcast.100
  198.0 0.7 reduce.5
  198.7 0.1 eq.85
  198.7 136.3 %all-to-all-done.2 = bf16[32,24,4096]{2,1,0:T(8,128)(2,1)} async-done(((bf16[32,24,4096]{2,1,0:T(8,128)(2,1)}), bf16[32,24,4096]{2,1,0:T(8,128)(2,1)}, u32[]{:S(2)}, u32[]{:S(2)}) %all-to-all-start.2) | async-done | bytes 6291488 | tf_op jit(solution)/shard_map/all_to_all | solution.py:62
  335.0 6.0 %fusion.9 = f32[192,4096]{1,0:T(8,128)} fusion(bf16[768,4096]{1,0:T(8,128)(2,1)} %bitcast.7, s32[768]{0:T(1024)S(1)} %eq.85), kind=kOutput, calls=%fused_computation.21 | convolution fusion | flops 1208107008 | bytes 9440256 | tf_op jit(solution)/shard_map/jr,jd->rd/dot_general | solution.py:72
  341.0 0.0 reduce-scatter.2.cloned.1.call-update
  341.0 2.8 multiply_convert_fusion
  343.9 67.9 %reduce-scatter.2.cloned.1.call-done = f32[192,256]{1,0:T(8,128)} async-done(((f32[192,4096]{1,0:T(8,128)}), f32[192,256]{1,0:T(8,128)}) %reduce-scatter.2.cloned.1.call-update) | async-done | bytes 196624 | tf_op jit(solution)/shard_map/reduce_scatter | solution.py:78
  (9 shorter events, 0.1 us)
Async XLA Ops:
  7.2 24.8 %copy-start = (bf16[192,4096]{1,0:T(8,128)(2,1)S(1)}, bf16[192,4096]{1,0:T(8,128)(2,1)}, u32[]{:S(2)}) copy-start(bf16[192,4096]{1,0:T(8,128)(2,1)} %param.9) | copy-start | bytes 4718596
  36.5 5.0 %copy-start.5 = (s32[128]{0:T(128)S(1)}, s32[128]{0:T(128)}, u32[]{:S(2)}) copy-start(s32[128]{0:T(128)} %param.8) | copy-start | bytes 1540
  36.5 5.1 %copy-start.2 = (bf16[4096]{0:T(1024)(128)(2,1)S(1)}, bf16[4096]{0:T(1024)(128)(2,1)}, u32[]{:S(2)}) copy-start(bf16[4096]{0:T(1024)(128)(2,1)} %param.10) | copy-start | bytes 24580
  36.5 140.9 %copy-start.3 = (bf16[128,4096]{1,0:T(8,128)(2,1)S(1)}, bf16[128,4096]{1,0:T(8,128)(2,1)}, u32[]{:S(2)}) copy-start(bf16[128,4096]{1,0:T(8,128)(2,1)} %param.6) | copy-start | bytes 3145732
  36.5 140.9 %all-to-all-start.1 = ((bf16[32,24,4096]{2,1,0:T(8,128)(2,1)}), bf16[32,24,4096]{2,1,0:T(8,128)(2,1)}, u32[]{:S(2)}, u32[]{:S(2)}) async-start(bf16[32,24,4096]{2,1,0:T(8,128)(2,1)} %convolution_convert_fusion.1), calls=%async_computation.1 | async-start | bytes 12582912 | tf_op jit(solution)/shard_map/all_to_all | solution.py:37
  177.4 4.9 %copy-start.4 = (bf16[128,4096]{1,0:T(8,128)(2,1)S(1)}, bf16[128,4096]{1,0:T(8,128)(2,1)}, u32[]{:S(2)}) copy-start(bf16[128,4096]{1,0:T(8,128)(2,1)} %param.11) | copy-start | bytes 3145732
  182.3 4.7 %copy-start.1 = (f32[128,4096]{1,0:T(8,128)}, f32[128,4096]{1,0:T(8,128)S(1)}, u32[]{:S(2)}) copy-start(f32[128,4096]{1,0:T(8,128)S(1)} %get-tuple-element.8) | copy-start | bytes 6291460
  187.0 148.0 %all-to-all-start.2 = ((bf16[32,24,4096]{2,1,0:T(8,128)(2,1)}), bf16[32,24,4096]{2,1,0:T(8,128)(2,1)}, u32[]{:S(2)}, u32[]{:S(2)}) async-start(bf16[32,24,4096]{2,1,0:T(8,128)(2,1)} %bitcast.29), calls=%async_computation.2 | async-start | bytes 12582912 | tf_op jit(solution)/shard_map/all_to_all | solution.py:62
  197.4 214.4 %reduce-scatter.2.cloned.1.call-start = ((), (), s32[]{:S(2)}) async-start(), calls=%async_computation.4 | async-start | bytes 3342336 | tf_op jit(solution)/shard_map/reduce_scatter | solution.py:78
Sparse Core Ops, SparseCore 0:
  341.1 70.6 reduce-scatter.1
where the time goes:
time: 421 us; the launch traced here: 419 us
  waiting for transfers between devices  340 us (81%)
  matrix products  20 us (5%)
  blocking collectives  18.9 us (4%)
  starting transfers between devices  15.5 us (4%)
  between operations  14.2 us (3%)
  other arithmetic  6 us (1%)
  local copies, waits for them, and re-layouts  4.33 us (1%)
    all_to_all x1, waiting for transfers between devices, per_device(): lax.all_to_all(slot_grad.reshape(table_size, capacity, features), 'table'...  136 us
    all_to_all x1, waiting for transfers between devices, per_device(): lax.all_to_all(lookup_result, 'table', split_axis=0, concat_axis=0, tiled...  136 us
    reduce_scatter x1, waiting for transfers between devices, per_device(): lax.psum_scatter(partial_sum, 'group', scatter_dimension=1, tiled=True)  67.9 us
    all_to_all x1, blocking collectives, per_device(): lax.all_to_all(request, 'table', split_axis=0, concat_axis=0, tiled=True)  18.9 us
    all_to_all x1, starting transfers between devices, per_device(): lax.all_to_all(slot_grad.reshape(table_size, capacity, features), 'table'...  10.4 us
  transfers between devices with their start and end apart: 3, of which 3 were waited for; matrix products, arithmetic and copies ran while one was open for 1% of the time, Pallas kernels for 0%

commit v1 on v0

v1 whole, which is shorter than its diff:
```python
import functools

import jax
import jax.numpy as jnp
from jax import lax
from jax.experimental import pallas as pl
from jax.experimental.pallas import tpu as pltpu
from jax.sharding import Mesh, PartitionSpec as P

Z, C, Y, X = 8, 2, 8, 4
G = ("z", "c")
T = ("y", "x")


def count_kernel(step, wide, a_ref, b_ref, out_ref):
    ngram = max(a_ref.shape[1], b_ref.shape[0])
    rows, cols = out_ref.shape

    def strip(i, carry):
        here = pl.ds(pl.multiple_of(i * step, step), step)
        a = a_ref[here, :]
        for j in range(0, cols, wide):
            b = b_ref[:, j : j + wide]
            total = None
            for k in range(ngram):
                ak = a[:, k : k + 1] if a.shape[1] > 1 else a
                bk = b[k : k + 1, :] if b.shape[0] > 1 else b
                term = jnp.where(ak == bk, 1.0, 0.0)
                total = term if total is None else total + term
            out_ref[here, j : j + wide] = total.astype(jnp.bfloat16)
        return carry

    lax.fori_loop(0, rows // step, strip, 0)


def count_matrix(a, b, block):
    rows, cols = a.shape[0], b.shape[1]
    return pl.pallas_call(
        functools.partial(count_kernel, 32, 512),
        grid=(rows // block,),
        in_specs=[
            pl.BlockSpec((block, a.shape[1]), lambda i: (i, 0)),
            pl.BlockSpec(b.shape, lambda i: (0, 0)),
        ],
        out_specs=pl.BlockSpec((block, cols), lambda i: (i, 0)),
        out_shape=jax.ShapeDtypeStruct((rows, cols), jnp.bfloat16),
        cost_estimate=pl.CostEstimate(
            flops=rows * cols * 12, bytes_accessed=rows * cols * 2, transcendentals=0
        ),
        compiler_params=pltpu.CompilerParams(vmem_limit_bytes=24 * 2**20),
    )(a, b)


def swap_core(v):
    return lax.ppermute(v, "c", [(0, 1), (1, 0)])


def both_cores(v):
    other = swap_core(v)
    first = lax.axis_index("c") == 0
    return jnp.concatenate([jnp.where(first, v, other), jnp.where(first, other, v)], axis=0)


def spread(v, n, axis):
    whole = jnp.broadcast_to(v[None], (n,) + v.shape)
    return lax.all_to_all(whole, axis, split_axis=0, concat_axis=0, tiled=True)


def to_features(v, blocks):
    tok, features = v.shape
    v = v.reshape(tok, blocks, features // blocks).transpose(1, 0, 2)
    v = lax.all_to_all(v, G, split_axis=0, concat_axis=0, tiled=True)
    return v.reshape(blocks * tok, features // blocks)


def per_device(embedded, ngram_ids, counts, slab, gain, cotangent):
    tok, features = embedded.shape
    ngram = ngram_ids.shape[1]
    rows = slab.shape[0]
    blocks = Z * C
    width = features // blocks
    all_rows = rows * Y * X
    all_tok = tok * blocks
    mine = lax.axis_index(G) * width
    here_x = lax.axis_index("x")

    piece = lax.dynamic_slice(slab, (0, mine), (rows, width))
    pieces = [piece] + [
        lax.ppermute(piece, "x", [(i, (i + s) % X) for i in range(X)]) for s in range(1, X)
    ]
    table = lax.all_gather(jnp.concatenate(pieces, axis=0), "y", tiled=True)
    from_x = (here_x - jnp.arange(X)) % X
    owner = jnp.arange(Y)[:, None] * X + from_x[None, :]
    table_row = (owner[:, :, None] * rows + jnp.arange(rows)).reshape(1, all_rows)
    owner = jnp.arange(X)[:, None] + jnp.arange(Y)[None, :] * X
    grad_row = (owner[:, :, None] * rows + jnp.arange(rows)).reshape(all_rows, 1)

    ids = jnp.where(jnp.arange(ngram)[:, None] < counts[None, :], ngram_ids.T, -1)
    ids = spread(both_cores(ids), Z, "z")
    ids = ids.reshape(blocks, ngram, tok).transpose(1, 0, 2).reshape(ngram, all_tok)
    count_f = jnp.sum((ids >= 0).astype(jnp.float32), axis=0)[:, None]
    hot = count_matrix(ids.T, table_row, 256)
    hot_t = count_matrix(grad_row, ids, 768)

    emb = to_features(embedded, blocks).astype(jnp.float32)
    cot = to_features(cotangent, blocks).astype(jnp.float32)
    gain_f = lax.dynamic_slice(gain, (mine,), (width,)).astype(jnp.float32)

    pooled = jnp.dot(hot, table, preferred_element_type=jnp.float32) / count_f
    hidden = emb + pooled
    grad_out = cot * gain_f
    sums = jnp.stack([jnp.sum(hidden * hidden, axis=1), jnp.sum(hidden * grad_out, axis=1)])
    sums = spread(sums.reshape(2 * all_tok // 128, 128), blocks, G)
    sums = jnp.sum(sums.reshape(blocks, 2, all_tok), axis=0) / features
    inv_rms = lax.rsqrt(sums[0] + 1e-05)[:, None]
    inner = sums[1][:, None]
    normed = (hidden * inv_rms * gain_f).astype(jnp.bfloat16)
    grad_hidden = inv_rms * grad_out - hidden * (inv_rms * inv_rms * inv_rms) * inner
    token_grad = (grad_hidden / count_f).astype(jnp.bfloat16)

    partial = jnp.dot(hot_t, token_grad, preferred_element_type=jnp.float32)
    column = lax.psum_scatter(
        partial.astype(jnp.bfloat16), "x", scatter_dimension=0, tiled=True
    )
    back = lax.all_to_all(
        normed.reshape(blocks, tok, width), G, split_axis=0, concat_axis=0, tiled=True
    )
    normed = back.transpose(1, 0, 2).reshape(tok, features)

    column = lax.all_to_all(
        column.reshape(Y, rows, width), "y", split_axis=0, concat_axis=0, tiled=True
    )
    row_grads = jnp.sum(column.astype(jnp.float32), axis=0)
    return (normed, row_grads)


def solution(mesh):
    fine = Mesh(mesh.devices.reshape(Z, C, Y, X), ("z", "c", "y", "x"))
    every = ("z", "c", "y", "x")
    in_specs = (P(every, None), P(every, None), P(every), P(T, None), P(), P(every, None))
    out_specs = (P(every, None), P(T, G))
    return jax.shard_map(
        per_device, mesh=fine, in_specs=in_specs, out_specs=out_specs, check_vma=False
    )
```

time: 421 us -> 287 us (0.68)
  waiting for transfers between devices: 340 us -> 65.3 us
  Pallas kernels: 0 us -> 55.8 us
  starting transfers between devices: 15.5 us -> 48.2 us
  local copies, waits for them, and re-layouts: 4.33 us -> 29.6 us
  blocking collectives: 18.9 us -> 35.6 us
  matrix products: 20 us -> 31.4 us
    all_to_all x2 -> x5, waiting for transfers between devices: 272 us -> 55.2 us  [the longest x2 26.9 us: to_features(): v = lax.all_to_all(v, G, split_axis=0, concat_axis=0, tiled=True)]
    reduce_scatter x1, waiting for transfers between devices: 67.9 us -> 6.77 us  [per_device(): lax.psum_scatter(partial.astype(jnp.bfloat16), 'x', scatter_dimension=0,...]
    pallas_call x0 -> x2, Pallas kernels: none -> 55.8 us  [count_matrix(): pl.pallas_call(functools.partial(count_kernel, 32, 512), grid=(rows // bl...]
    unnamed x12 -> x14, local copies, waits for them, and re-layouts: 0.03 us -> 19.8 us
    ppermute x0 -> x4, starting transfers between devices: none -> 18.6 us  [the longest x3 11.4 us: per_device(): lax.ppermute(piece, 'x', [(i, (i + s) % X) for i in range(X)])]
    all_to_all x1, blocking collectives: 18.9 us -> 35.6 us  [per_device(): lax.all_to_all(normed.reshape(blocks, tok, width), G, split_axis=0, conca...]
    all_to_all x2 -> x5, starting transfers between devices: 15.4 us -> 29.3 us  [the longest x2 13.3 us: spread(): return lax.all_to_all(whole, axis, split_axis=0, concat_axis=0, tiled=True)]
    dot_general x4 -> x2, matrix products: 20 us -> 31.4 us  [the longest x1 17.5 us: per_device(): partial = jnp.dot(hot_t, token_grad, preferred_element_type=jnp.float32)]
  transfers between devices with their start and end apart: 3 -> 11, of which waited for: 3 -> 6; matrix products, arithmetic and copies ran while one was open for 1% -> 5% of each run, Pallas kernels for 0% -> 20%
where the time goes in v1:
time: 287 us; the launch traced here: 286 us
  waiting for transfers between devices  65.3 us (23%)
  Pallas kernels  55.8 us (19%)
  starting transfers between devices  48.2 us (17%)
  blocking collectives  35.6 us (12%)
  matrix products  31.4 us (11%)
  local copies, waits for them, and re-layouts  29.6 us (10%)
  between operations  14.3 us (5%)
  other arithmetic  5.98 us (2%)
    pallas_call x2, Pallas kernels, count_matrix(): pl.pallas_call(functools.partial(count_kernel, 32, 512), grid=(rows // bl...  55.8 us
    all_to_all x1, blocking collectives, per_device(): lax.all_to_all(normed.reshape(blocks, tok, width), G, split_axis=0, conca...  35.6 us
    all_to_all x2, waiting for transfers between devices, to_features(): v = lax.all_to_all(v, G, split_axis=0, concat_axis=0, tiled=True)  26.9 us
    all_to_all x1, waiting for transfers between devices, per_device(): lax.all_to_all(column.reshape(Y, rows, width), 'y', split_axis=0, concat_...  22.5 us
    unnamed x14, local copies, waits for them, and re-layouts  19.8 us
    dot_general x1, matrix products, per_device(): partial = jnp.dot(hot_t, token_grad, preferred_element_type=jnp.float32)  17.5 us
    dot_general x1, matrix products, per_device(): pooled = jnp.dot(hot, table, preferred_element_type=jnp.float32) / count_f  14 us
    all_to_all x2, starting transfers between devices, spread(): return lax.all_to_all(whole, axis, split_axis=0, concat_axis=0, tiled=True)  13.3 us
  transfers between devices with their start and end apart: 11, of which 6 were waited for; matrix products, arithmetic and copies ran while one was open for 5% of the time, Pallas kernels for 20%

profile of v1, /device:TPU:1, one launch (start us, length us, event | category | flops | bytes accessed | tf_op | source)
XLA Modules:
  0.0 286.2 jit_solution(4748540283656348113)
XLA Ops:
  7.2 0.0 copy-start
  7.2 0.0 copy-start.5
  7.2 0.0 all-gather.2.cloned.1.call-start
  7.2 1.3 copy-done
  8.6 3.9 %collective-permute-start.1 = (bf16[192,256]{1,0:T(8,128)(2,1)S(1)}, bf16[192,256]{1,0:T(8,128)(2,1)S(1)}, u32[]{:S(2)}, u32[]{:S(2)}) collective-permute-start(bf16[192,256]{1,0:T(8,128)(2,1)S(1)} %constant_dynamic-slice_fusion), channel_id=1, source_target_pairs={{0,1},{1,2},{2,3},{3,0},{4,5},{5,6},{6,7},{7,4},{8,9},{9,10},{10,1... | collective-permute-start | bytes 294920 | tf_op jit(solution)/shard_map/ppermute | solution.py:89
  12.6 4.4 %collective-permute-start.2 = (bf16[192,256]{1,0:T(8,128)(2,1)S(1)}, bf16[192,256]{1,0:T(8,128)(2,1)S(1)}, u32[]{:S(2)}, u32[]{:S(2)}) collective-permute-start(bf16[192,256]{1,0:T(8,128)(2,1)S(1)} %constant_dynamic-slice_fusion), channel_id=1, source_target_pairs={{0,2},{1,3},{2,0},{3,1},{4,6},{5,7},{6,4},{7,5},{8,10},{9,11},{10,... | collective-permute-start | bytes 294920 | tf_op jit(solution)/shard_map/ppermute | solution.py:89
  16.9 3.1 %collective-permute-start.3 = (bf16[192,256]{1,0:T(8,128)(2,1)S(1)}, bf16[192,256]{1,0:T(8,128)(2,1)S(1)}, u32[]{:S(2)}, u32[]{:S(2)}) collective-permute-start(bf16[192,256]{1,0:T(8,128)(2,1)S(1)} %constant_dynamic-slice_fusion), channel_id=1, source_target_pairs={{0,3},{1,0},{2,1},{3,2},{4,7},{5,4},{6,5},{7,6},{8,11},{9,8},{10,9... | collective-permute-start | bytes 294920 | tf_op jit(solution)/shard_map/ppermute | solution.py:89
  20.0 0.0 collective-permute-done.1
  20.0 0.0 collective-permute-done.2
  20.0 2.6 collective-permute-done.3
  22.6 0.8 pad_maximum_fusion
  23.4 0.0 all-gather.2.cloned.1.call-update
  23.4 0.7 bitcast_select_fusion
  24.1 7.2 %collective-permute-start = (s32[4,128]{1,0:T(4,128)S(1)}, s32[4,128]{1,0:T(4,128)S(1)}, u32[]{:S(2)}, u32[]{:S(2)}) collective-permute-start(s32[4,128]{1,0:T(4,128)S(1)} %bitcast_select_fusion), channel_id=1, source_target_pairs={{0,32},{32,0},{1,33},{33,1},{2,34},{34,2},{3,35},{35,3},{4,36},{36... | collective-permute-start | bytes 6152 | tf_op jit(solution)/shard_map/ppermute | solution.py:55
  31.3 0.8 collective-permute-done
  32.1 0.7 broadcast_select_fusion.1
  32.8 0.6 broadcast_in_dim.10
  33.4 6.8 %all-to-all-start.1 = ((s32[8,8,128]{2,1,0:T(8,128)}), s32[8,8,128]{2,1,0:T(8,128)S(1)}, u32[]{:S(2)}, u32[]{:S(2)}) async-start(s32[8,8,128]{2,1,0:T(8,128)} %broadcast_in_dim.10), calls=%async_computation.1 | async-start | bytes 65536 | tf_op jit(solution)/shard_map/all_to_all | solution.py:66
  40.2 0.0 copy-done.5
  40.2 0.0 copy-start.6
  40.3 1.1 copy.27
  41.3 5.8 %all-to-all-done.1 = s32[8,8,128]{2,1,0:T(8,128)S(1)} async-done(((s32[8,8,128]{2,1,0:T(8,128)}), s32[8,8,128]{2,1,0:T(8,128)S(1)}, u32[]{:S(2)}, u32[]{:S(2)}) %all-to-all-start.1) | async-done | bytes 32800 | tf_op jit(solution)/shard_map/all_to_all | solution.py:66
  47.1 5.2 %all-to-all-start.2 = ((bf16[16,128,256]{2,1,0:T(8,128)(2,1)}), bf16[16,128,256]{2,1,0:T(8,128)(2,1)S(1)}, u32[]{:S(2)}, u32[]{:S(2)}) async-start(bf16[16,128,256]{2,1,0:T(8,128)(2,1)} %bitcast.44), calls=%async_computation.2 | async-start | bytes 2097152 | tf_op jit(solution)/shard_map/all_to_all | solution.py:72
  52.3 0.0 copy-done.6
  52.3 1.1 copy.28
  53.4 26.9 %all-to-all-done.2 = bf16[16,128,256]{2,1,0:T(8,128)(2,1)S(1)} async-done(((bf16[16,128,256]{2,1,0:T(8,128)(2,1)}), bf16[16,128,256]{2,1,0:T(8,128)(2,1)S(1)}, u32[]{:S(2)}, u32[]{:S(2)}) %all-to-all-start.2) | async-done | bytes 1048608 | tf_op jit(solution)/shard_map/all_to_all | solution.py:72
  80.3 4.2 %all-to-all-start = ((bf16[16,128,256]{2,1,0:T(8,128)(2,1)}), bf16[16,128,256]{2,1,0:T(8,128)(2,1)}, u32[]{:S(2)}, u32[]{:S(2)}) async-start(bf16[16,128,256]{2,1,0:T(8,128)(2,1)} %bitcast.46), calls=%async_computation | async-start | bytes 2097152 | tf_op jit(solution)/shard_map/all_to_all | solution.py:72
  84.6 0.1 add_multiply_fusion
  84.7 0.1 iota_add_fusion.1
  84.7 0.1 add.124.b_ref
  84.8 0.8 dynamic-slice_convert_fusion
  85.6 0.4 copy.18.a_ref
  86.0 23.4 %shard_map.77 = bf16[2048,6144]{1,0:T(8,128)(2,1)S(1)} custom-call(s32[2048,4]{1,0:T(8,128)S(1)} %copy.18.a_ref, s32[1,6144]{1,0:T(1,128)S(1)} %add.124.b_ref), custom_call_target="tpu_custom_call" | custom-call | flops 150994944 | bytes 25165824 | tf_op jit(solution)/shard_map/pallas_call | solution.py:38
  109.4 0.0 copy-start.3
  109.4 8.3 %copy-done.3 = bf16[2048,6144]{1,0:T(8,128)(2,1)} copy-done((bf16[2048,6144]{1,0:T(8,128)(2,1)}, bf16[2048,6144]{1,0:T(8,128)(2,1)S(1)}, u32[]{:S(2)}) %copy-start.3) | copy-done | bytes 25165848
  117.7 0.0 all-to-all-done
  117.8 0.0 all-gather.2.cloned.1.call-done
  117.8 14.0 %multiply_reduce_fusion = (f32[2048]{0:T(1024)S(1)}, f32[2048]{0:T(1024)S(1)}, f32[2048,256]{1,0:T(8,128)}) fusion(f32[256]{0:T(256)S(1)} %dynamic-slice_convert_fusion, bf16[16,128,256]{2,1,0:T(8,128)(2,1)S(1)} %all-to-all-done.2, f32[2048]{0:T(1024)S(1)} %bitcast.57, bf16[2048,6144]{1,0:T(8,128)(2,1)} %copy-done.3, ...), kind=kOutput, calls=%fused_computation.10 | convolution fusion | flops 6447165440 | bytes 32531456 | tf_op jit(solution)/shard_map/dot_general | solution.py:109
  131.8 0.7 broadcast_in_dim.13
  132.5 6.5 %all-to-all-start.3 = ((f32[16,32,128]{2,1,0:T(8,128)}), f32[16,32,128]{2,1,0:T(8,128)S(1)}, u32[]{:S(2)}, u32[]{:S(2)}) async-start(f32[16,32,128]{2,1,0:T(8,128)} %broadcast_in_dim.13), calls=%async_computation.3 | async-start | bytes 524288 | tf_op jit(solution)/shard_map/all_to_all | solution.py:66
  139.0 0.2 reduce-scatter.2.cloned.1.call-start
  139.2 0.1 iota_add_fusion
  139.3 4.7 %add.137.a_ref = s32[6144,1]{1,0:T(8,128)} reshape(s32[4,8,192]{2,1,0:T(8,128)S(1)} %iota_add_fusion) | data formatting | bytes 49152 | tf_op jit(solution)/shard_map/add | solution.py:96
  144.0 0.0 copy-start.4
  144.0 1.9 copy-done.4
  145.9 32.4 %shard_map.78 = bf16[6144,2048]{1,0:T(8,128)(2,1)S(1)} custom-call(s32[6144,1]{1,0:T(8,128)S(1)} %copy-done.4, s32[4,2048]{1,0:T(4,128)S(1)} %bitcast.49), custom_call_target="tpu_custom_call" | custom-call | flops 150994944 | bytes 25165824 | tf_op jit(solution)/shard_map/pallas_call | solution.py:38
  178.3 0.0 copy-start.2
  178.3 8.3 %copy-done.2 = bf16[6144,2048]{1,0:T(8,128)(2,1)} copy-done((bf16[6144,2048]{1,0:T(8,128)(2,1)}, bf16[6144,2048]{1,0:T(8,128)(2,1)S(1)}, u32[]{:S(2)}) %copy-start.2) | copy-done | bytes 25165848
  186.6 0.0 all-to-all-done.3
  186.7 17.5 %convolution_convert_fusion = bf16[6144,256]{1,0:T(8,128)(2,1)} fusion(bf16[6144,2048]{1,0:T(8,128)(2,1)} %copy-done.2, f32[2048,256]{1,0:T(8,128)} %get-tuple-element.8, bf16[2048,256]{1,0:T(8,128)(2,1)S(1)} %bitcast.54, f32[2048]{0:T(1024)S(1)} %get-tuple-element.4, f32[2048]{0:T(1024)S(1)} %multiply_multiply_fusion, f32[2048]{0:T(1024)S(1)} %get-tuple-element.5, ...), kind=kOutput, calls=%fused_computation | convolution fusion | flops 6448218112 | bytes 31491072 | tf_op jit(solution)/shard_map/dot_general | solution.py:121
  204.1 0.0 reduce-scatter.2.cloned.1.call-update
  204.2 1.9 multiply_convert_fusion
  206.1 35.6 %all_to_all.30 = bf16[16,128,256]{2,1,0:T(8,128)(2,1)S(1)} all-to-all(bf16[16,128,256]{2,1,0:T(8,128)(2,1)S(1)} %bitcast.51), channel_id=1, replica_groups=mesh['z'=8,'c'=2,'y'=8,'x'=4] {'z','c'}, dimensions={0} | all-to-all | bytes 2097152 | tf_op jit(solution)/shard_map/all_to_all | solution.py:125
  241.7 6.8 %reduce-scatter.2.cloned.1.call-done = bf16[1536,256]{1,0:T(8,128)(2,1)} async-done(((bf16[6144,256]{1,0:T(8,128)(2,1)}), bf16[1536,256]{1,0:T(8,128)(2,1)}) %reduce-scatter.2.cloned.1.call-update) | async-done | bytes 786448 | tf_op jit(solution)/shard_map/reduce_scatter | solution.py:122
  248.4 0.0 copy-start.1
  248.5 6.6 %all-to-all-start.5 = ((bf16[8,192,256]{2,1,0:T(8,128)(2,1)}), bf16[8,192,256]{2,1,0:T(8,128)(2,1)S(1)}, u32[]{:S(2)}, u32[]{:S(2)}) async-start(bf16[8,192,256]{2,1,0:T(8,128)(2,1)} %bitcast.56), calls=%async_computation.6 | async-start | bytes 1572864 | tf_op jit(solution)/shard_map/all_to_all | solution.py:130
  255.0 1.1 copy.24
  256.1 22.5 %all-to-all-done.5 = bf16[8,192,256]{2,1,0:T(8,128)(2,1)S(1)} async-done(((bf16[8,192,256]{2,1,0:T(8,128)(2,1)}), bf16[8,192,256]{2,1,0:T(8,128)(2,1)S(1)}, u32[]{:S(2)}, u32[]{:S(2)}) %all-to-all-start.5) | async-done | bytes 786464 | tf_op jit(solution)/shard_map/all_to_all | solution.py:130
  278.6 0.8 convert_reduce_fusion
  279.4 0.0 copy-done.1
  (12 shorter events, 0.1 us)
Async XLA Ops:
  7.2 1.4 copy-start
  7.2 33.1 %copy-start.5 = (bf16[128,4096]{1,0:T(8,128)(2,1)S(1)}, bf16[128,4096]{1,0:T(8,128)(2,1)}, u32[]{:S(2)}) copy-start(bf16[128,4096]{1,0:T(8,128)(2,1)} %param.11) | copy-start | bytes 3145732
  7.2 110.6 %all-gather.2.cloned.1.call-start = ((), (), s32[]{:S(2)}) async-start(), calls=%async_computation.7 | async-start | bytes 3538944 | tf_op jit(solution)/shard_map/all_gather | solution.py:91
  8.6 11.4 %collective-permute-start.1 = (bf16[192,256]{1,0:T(8,128)(2,1)S(1)}, bf16[192,256]{1,0:T(8,128)(2,1)S(1)}, u32[]{:S(2)}, u32[]{:S(2)}) collective-permute-start(bf16[192,256]{1,0:T(8,128)(2,1)S(1)} %constant_dynamic-slice_fusion), channel_id=1, source_target_pairs={{0,1},{1,2},{2,3},{3,0},{4,5},{5,6},{6,7},{7,4},{8,9},{9,10},{10,1... | collective-permute-start | bytes 294920 | tf_op jit(solution)/shard_map/ppermute | solution.py:89
  12.6 7.4 %collective-permute-start.2 = (bf16[192,256]{1,0:T(8,128)(2,1)S(1)}, bf16[192,256]{1,0:T(8,128)(2,1)S(1)}, u32[]{:S(2)}, u32[]{:S(2)}) collective-permute-start(bf16[192,256]{1,0:T(8,128)(2,1)S(1)} %constant_dynamic-slice_fusion), channel_id=1, source_target_pairs={{0,2},{1,3},{2,0},{3,1},{4,6},{5,7},{6,4},{7,5},{8,10},{9,11},{10,... | collective-permute-start | bytes 294920 | tf_op jit(solution)/shard_map/ppermute | solution.py:89
  16.9 5.7 %collective-permute-start.3 = (bf16[192,256]{1,0:T(8,128)(2,1)S(1)}, bf16[192,256]{1,0:T(8,128)(2,1)S(1)}, u32[]{:S(2)}, u32[]{:S(2)}) collective-permute-start(bf16[192,256]{1,0:T(8,128)(2,1)S(1)} %constant_dynamic-slice_fusion), channel_id=1, source_target_pairs={{0,3},{1,0},{2,1},{3,2},{4,7},{5,4},{6,5},{7,6},{8,11},{9,8},{10,9... | collective-permute-start | bytes 294920 | tf_op jit(solution)/shard_map/ppermute | solution.py:89
  24.1 8.0 %collective-permute-start = (s32[4,128]{1,0:T(4,128)S(1)}, s32[4,128]{1,0:T(4,128)S(1)}, u32[]{:S(2)}, u32[]{:S(2)}) collective-permute-start(s32[4,128]{1,0:T(4,128)S(1)} %bitcast_select_fusion), channel_id=1, source_target_pairs={{0,32},{32,0},{1,33},{33,1},{2,34},{34,2},{3,35},{35,3},{4,36},{36... | collective-permute-start | bytes 6152 | tf_op jit(solution)/shard_map/ppermute | solution.py:55
  33.4 13.7 %all-to-all-start.1 = ((s32[8,8,128]{2,1,0:T(8,128)}), s32[8,8,128]{2,1,0:T(8,128)S(1)}, u32[]{:S(2)}, u32[]{:S(2)}) async-start(s32[8,8,128]{2,1,0:T(8,128)} %broadcast_in_dim.10), calls=%async_computation.1 | async-start | bytes 65536 | tf_op jit(solution)/shard_map/all_to_all | solution.py:66
  40.2 12.1 %copy-start.6 = (bf16[128,4096]{1,0:T(8,128)(2,1)S(1)}, bf16[128,4096]{1,0:T(8,128)(2,1)}, u32[]{:S(2)}) copy-start(bf16[128,4096]{1,0:T(8,128)(2,1)} %param.6) | copy-start | bytes 3145732
  47.1 33.2 %all-to-all-start.2 = ((bf16[16,128,256]{2,1,0:T(8,128)(2,1)}), bf16[16,128,256]{2,1,0:T(8,128)(2,1)S(1)}, u32[]{:S(2)}, u32[]{:S(2)}) async-start(bf16[16,128,256]{2,1,0:T(8,128)(2,1)} %bitcast.44), calls=%async_computation.2 | async-start | bytes 2097152 | tf_op jit(solution)/shard_map/all_to_all | solution.py:72
  80.3 37.4 %all-to-all-start = ((bf16[16,128,256]{2,1,0:T(8,128)(2,1)}), bf16[16,128,256]{2,1,0:T(8,128)(2,1)}, u32[]{:S(2)}, u32[]{:S(2)}) async-start(bf16[16,128,256]{2,1,0:T(8,128)(2,1)} %bitcast.46), calls=%async_computation | async-start | bytes 2097152 | tf_op jit(solution)/shard_map/all_to_all | solution.py:72
  109.4 8.3 %copy-start.3 = (bf16[2048,6144]{1,0:T(8,128)(2,1)}, bf16[2048,6144]{1,0:T(8,128)(2,1)S(1)}, u32[]{:S(2)}) copy-start(bf16[2048,6144]{1,0:T(8,128)(2,1)S(1)} %shard_map.77) | copy-start | bytes 75497472
  132.5 54.1 %all-to-all-start.3 = ((f32[16,32,128]{2,1,0:T(8,128)}), f32[16,32,128]{2,1,0:T(8,128)S(1)}, u32[]{:S(2)}, u32[]{:S(2)}) async-start(f32[16,32,128]{2,1,0:T(8,128)} %broadcast_in_dim.13), calls=%async_computation.3 | async-start | bytes 524288 | tf_op jit(solution)/shard_map/all_to_all | solution.py:66
  139.0 109.4 %reduce-scatter.2.cloned.1.call-start = ((), (), s32[]{:S(2)}) async-start(), calls=%async_computation.8 | async-start | bytes 3932160 | tf_op jit(solution)/shard_map/reduce_scatter | solution.py:122
  144.0 1.9 copy-start.4
  178.3 8.3 %copy-start.2 = (bf16[6144,2048]{1,0:T(8,128)(2,1)}, bf16[6144,2048]{1,0:T(8,128)(2,1)S(1)}, u32[]{:S(2)}) copy-start(bf16[6144,2048]{1,0:T(8,128)(2,1)S(1)} %shard_map.78) | copy-start | bytes 75497472
  248.4 31.0 %copy-start.1 = (bf16[192,4096]{1,0:T(8,128)(2,1)S(1)}, bf16[192,4096]{1,0:T(8,128)(2,1)}, u32[]{:S(2)}) copy-start(bf16[192,4096]{1,0:T(8,128)(2,1)} %param.9) | copy-start | bytes 4718596
  248.5 30.2 %all-to-all-start.5 = ((bf16[8,192,256]{2,1,0:T(8,128)(2,1)}), bf16[8,192,256]{2,1,0:T(8,128)(2,1)S(1)}, u32[]{:S(2)}, u32[]{:S(2)}) async-start(bf16[8,192,256]{2,1,0:T(8,128)(2,1)} %bitcast.56), calls=%async_computation.6 | async-start | bytes 1572864 | tf_op jit(solution)/shard_map/all_to_all | solution.py:130
Sparse Core Ops, SparseCore 0:
  23.5 52.5 all-gather.1
  204.3 44.1 reduce-scatter.1

commit v2 on v1

--- a/solution.py
+++ b/solution.py
@@ -10,6 +10,7 @@
 Z, C, Y, X = 8, 2, 8, 4
 G = ("z", "c")
 T = ("y", "x")
+ROWS_Y = 80
 
 
 def count_kernel(step, wide, a_ref, b_ref, out_ref):
@@ -51,14 +52,8 @@
     )(a, b)
 
 
-def swap_core(v):
-    return lax.ppermute(v, "c", [(0, 1), (1, 0)])
-
-
-def both_cores(v):
-    other = swap_core(v)
-    first = lax.axis_index("c") == 0
-    return jnp.concatenate([jnp.where(first, v, other), jnp.where(first, other, v)], axis=0)
+def shift(s):
+    return [(i, (i + s) % X) for i in range(X)]
 
 
 def spread(v, n, axis):
@@ -66,11 +61,15 @@
     return lax.all_to_all(whole, axis, split_axis=0, concat_axis=0, tiled=True)
 
 
-def to_features(v, blocks):
-    tok, features = v.shape
-    v = v.reshape(tok, blocks, features // blocks).transpose(1, 0, 2)
-    v = lax.all_to_all(v, G, split_axis=0, concat_axis=0, tiled=True)
-    return v.reshape(blocks * tok, features // blocks)
+def two_runs(v):
+    late = v[:, :, ROWS_Y:].transpose(1, 0, 2, 3)
+    return v[:, :, :ROWS_Y].reshape(-1, v.shape[3]), late.reshape(-1, v.shape[3])
+
+
+def rows_of(hot, token_grad):
+    return lax.dot_general(
+        hot, token_grad, (((0,), (0,)), ((), ())), preferred_element_type=jnp.float32
+    )
 
 
 def per_device(embedded, ngram_ids, counts, slab, gain, cotangent):
@@ -84,30 +83,37 @@
     mine = lax.axis_index(G) * width
     here_x = lax.axis_index("x")
 
+    ids = jnp.where(jnp.arange(ngram)[:, None] < counts[None, :], ngram_ids.T, -1)
+    ids = spread(ids, blocks, G)
+    ids, embedded, cotangent = lax.optimization_barrier((ids, embedded, cotangent))
+    ids = ids.transpose(0, 2, 1).reshape(all_tok, ngram)
+
+    sent = jnp.concatenate([embedded, cotangent], axis=0)
+    sent = sent.reshape(2 * tok, blocks, width).transpose(1, 0, 2)
+    came = lax.all_to_all(sent, G, split_axis=0, concat_axis=0, tiled=True)
+
     piece = lax.dynamic_slice(slab, (0, mine), (rows, width))
-    pieces = [piece] + [
-        lax.ppermute(piece, "x", [(i, (i + s) % X) for i in range(X)]) for s in range(1, X)
-    ]
+    pieces = [piece] + [lax.ppermute(piece, "x", shift(s)) for s in range(1, X)]
     table = lax.all_gather(jnp.concatenate(pieces, axis=0), "y", tiled=True)
     from_x = (here_x - jnp.arange(X)) % X
     owner = jnp.arange(Y)[:, None] * X + from_x[None, :]
-    table_row = (owner[:, :, None] * rows + jnp.arange(rows)).reshape(1, all_rows)
-    owner = jnp.arange(X)[:, None] + jnp.arange(Y)[None, :] * X
-    grad_row = (owner[:, :, None] * rows + jnp.arange(rows)).reshape(all_rows, 1)
+    table_row = owner[:, :, None] * rows + jnp.arange(rows)
+    table_y, table_x = two_runs(table.reshape(Y, X, rows, width))
+    row_y, row_x = two_runs(table_row[..., None])
 
-    ids = jnp.where(jnp.arange(ngram)[:, None] < counts[None, :], ngram_ids.T, -1)
-    ids = spread(both_cores(ids), Z, "z")
-    ids = ids.reshape(blocks, ngram, tok).transpose(1, 0, 2).reshape(ngram, all_tok)
-    count_f = jnp.sum((ids >= 0).astype(jnp.float32), axis=0)[:, None]
-    hot = count_matrix(ids.T, table_row, 256)
-    hot_t = count_matrix(grad_row, ids, 768)
+    count_f = jnp.sum((ids >= 0).astype(jnp.float32), axis=1, keepdims=True)
+    hot_x = count_matrix(ids, row_x.T, 256)
+    hot_x, ids = lax.optimization_barrier((hot_x, ids))
+    hot_y = count_matrix(ids, row_y.T, 256)
 
-    emb = to_features(embedded, blocks).astype(jnp.float32)
-    cot = to_features(cotangent, blocks).astype(jnp.float32)
     gain_f = lax.dynamic_slice(gain, (mine,), (width,)).astype(jnp.float32)
 
-    pooled = jnp.dot(hot, table, preferred_element_type=jnp.float32) / count_f
-    hidden = emb + pooled
+    pooled = jnp.dot(hot_x, table_x, preferred_element_type=jnp.float32)
+    pooled = pooled + jnp.dot(hot_y, table_y, preferred_element_type=jnp.float32)
+    pooled, came = lax.optimization_barrier((pooled, came))
+    emb = came[:, :tok].reshape(all_tok, width).astype(jnp.float32)
+    cot = came[:, tok:].reshape(all_tok, width).astype(jnp.float32)
+    hidden = emb + pooled / count_f
     grad_out = cot * gain_f
     sums = jnp.stack([jnp.sum(hidden * hidden, axis=1), jnp.sum(hidden * grad_out, axis=1)])
     sums = spread(sums.reshape(2 * all_tok // 128, 128), blocks, G)
@@ -116,21 +122,35 @@
     inner = sums[1][:, None]
     normed = (hidden * inv_rms * gain_f).astype(jnp.bfloat16)
     grad_hidden = inv_rms * grad_out - hidden * (inv_rms * inv_rms * inv_rms) * inner
-    token_grad = (grad_hidden / count_f).astype(jnp.bfloat16)
+    token_grad = lax.optimization_barrier((grad_hidden / count_f).astype(jnp.bfloat16))
 
-    partial = jnp.dot(hot_t, token_grad, preferred_element_type=jnp.float32)
-    column = lax.psum_scatter(
-        partial.astype(jnp.bfloat16), "x", scatter_dimension=0, tiled=True
-    )
+    by_y = rows_of(hot_y, token_grad)
+    by_y, token_grad = lax.optimization_barrier((by_y, token_grad))
+    by_y = lax.psum_scatter(by_y, "y", scatter_dimension=0, tiled=True)
+
+    run = Y * (rows - ROWS_Y)
+    by_x = []
+    for s in (2, 1, 3, 0):
+        part = rows_of(hot_x[:, s * run : (s + 1) * run], token_grad)
+        if s:
+            part = part.astype(jnp.bfloat16)
+        part, token_grad = lax.optimization_barrier((part, token_grad))
+        if s:
+            part = lax.ppermute(part, "x", shift(-s)).astype(jnp.float32)
+        by_x.append(part)
+    by_x = sum(by_x[::-1]).astype(jnp.bfloat16).reshape(Y, rows - ROWS_Y, width)
+
     back = lax.all_to_all(
         normed.reshape(blocks, tok, width), G, split_axis=0, concat_axis=0, tiled=True
     )
+
+    by_x, back = lax.optimization_barrier((by_x, back))
     normed = back.transpose(1, 0, 2).reshape(tok, features)
-
-    column = lax.all_to_all(
-        column.reshape(Y, rows, width), "y", split_axis=0, concat_axis=0, tiled=True
-    )
-    row_grads = jnp.sum(column.astype(jnp.float32), axis=0)
+    by_x = lax.all_to_all(by_x, "y", split_axis=0, concat_axis=0, tiled=True)
+    by_x = jnp.sum(by_x.astype(jnp.float32), axis=0)
+    by_y = by_y.reshape(X, ROWS_Y, width)
+    by_y = by_y[0] + sum(lax.ppermute(by_y[s], "x", shift(-s)) for s in range(1, X))
+    row_grads = jnp.concatenate([by_y, by_x], axis=0)
     return (normed, row_grads)
 
 

time: 287 us -> 219 us (0.76)
  waiting for transfers between devices: 65.3 us -> 28.5 us
  Pallas kernels: 55.8 us -> 28 us
  blocking collectives: 35.6 us -> 18.8 us
  starting transfers between devices: 48.2 us -> 58.3 us
  local copies, waits for them, and re-layouts: 29.6 us -> 22.4 us
  other arithmetic: 5.98 us -> 12.6 us
    all_to_all x3, waiting for transfers between devices: 49.4 us -> 3.02 us  [the longest x1 3.01 us: per_device(): by_x = lax.all_to_all(by_x, 'y', split_axis=0, concat_axis=0, tiled=True)]
    pallas_call x2, Pallas kernels: 55.8 us -> 28 us  [count_matrix(): pl.pallas_call(functools.partial(count_kernel, 32, 512), grid=(rows // bl...]
    all_to_all x1, blocking collectives: 35.6 us -> 18.8 us  [spread(): return lax.all_to_all(whole, axis, split_axis=0, concat_axis=0, tiled=True)]
    ppermute x4 -> x9, waiting for transfers between devices: 3.36 us -> 18.1 us  [the longest x3 13.6 us: per_device(): part = lax.ppermute(part, 'x', shift(-s)).astype(jnp.float32)]
    ppermute x4 -> x9, starting transfers between devices: 18.6 us -> 30.8 us  [the longest x3 11.4 us: per_device(): pieces = [piece] + [lax.ppermute(piece, 'x', shift(s)) for s in range(1, X)]]
    unnamed x14 -> x20, local copies, waits for them, and re-layouts: 19.8 us -> 12.4 us
    reduce_scatter x1, waiting for transfers between devices: 6.77 us -> 0.01 us  [per_device(): by_y = lax.psum_scatter(by_y, 'y', scatter_dimension=0, tiled=True)]
    add x2 -> x0, local copies, waits for them, and re-layouts: 4.77 us -> none  [per_device(): owner[:, :, None] * rows + jnp.arange(rows)]
  transfers between devices with their start and end apart: 11 -> 15, of which waited for: 6 -> 6; matrix products, arithmetic and copies ran while one was open for 5% -> 17% of each run, Pallas kernels for 20% -> 13%
where the time goes in v2:
time: 219 us; the launch traced here: 217 us
  starting transfers between devices  58.3 us (27%)
  matrix products  33.6 us (15%)
  waiting for transfers between devices  28.5 us (13%)
  Pallas kernels  28 us (13%)
  local copies, waits for them, and re-layouts  22.4 us (10%)
  blocking collectives  18.8 us (9%)
  between operations  14.4 us (7%)
  other arithmetic  12.6 us (6%)
    pallas_call x2, Pallas kernels, count_matrix(): pl.pallas_call(functools.partial(count_kernel, 32, 512), grid=(rows // bl...  28 us
    dot_general x5, matrix products, rows_of(): lax.dot_general(hot, token_grad, (((0,), (0,)), ((), ())), preferred_elem...  21.8 us
    all_to_all x1, blocking collectives, spread(): return lax.all_to_all(whole, axis, split_axis=0, concat_axis=0, tiled=True)  18.8 us
    ppermute x3, waiting for transfers between devices, per_device(): part = lax.ppermute(part, 'x', shift(-s)).astype(jnp.float32)  13.6 us
    unnamed x20, local copies, waits for them, and re-layouts  12.4 us
    all_to_all x1, starting transfers between devices, spread(): return lax.all_to_all(whole, axis, split_axis=0, concat_axis=0, tiled=True)  12.4 us
    ppermute x3, starting transfers between devices, per_device(): pieces = [piece] + [lax.ppermute(piece, 'x', shift(s)) for s in range(1, X)]  11.4 us
    ppermute x3, starting transfers between devices, per_device(): lax.ppermute(by_y[s], 'x', shift(-s))  10.1 us
  transfers between devices with their start and end apart: 15, of which 6 were waited for; matrix products, arithmetic and copies ran while one was open for 17% of the time, Pallas kernels for 13%

profile of v2, /device:TPU:1, one launch (start us, length us, event | category | flops | bytes accessed | tf_op | source)
XLA Modules:
  0.0 216.8 jit_solution(17828356762187797716)
XLA Ops:
  7.2 0.0 all-gather.2.cloned.1.call-start
  7.2 1.3 copy-done
  8.6 3.9 %collective-permute-start = (bf16[192,256]{1,0:T(8,128)(2,1)S(1)}, bf16[192,256]{1,0:T(8,128)(2,1)S(1)}, u32[]{:S(2)}, u32[]{:S(2)}) collective-permute-start(bf16[192,256]{1,0:T(8,128)(2,1)S(1)} %constant_dynamic-slice_fusion), channel_id=1, source_target_pairs={{0,1},{1,2},{2,3},{3,0},{4,5},{5,6},{6,7},{7,4},{8,9},{9,10},{10,1... | collective-permute-start | bytes 294920 | tf_op jit(solution)/shard_map/ppermute | solution.py:96
  12.6 4.4 %collective-permute-start.1 = (bf16[192,256]{1,0:T(8,128)(2,1)S(1)}, bf16[192,256]{1,0:T(8,128)(2,1)S(1)}, u32[]{:S(2)}, u32[]{:S(2)}) collective-permute-start(bf16[192,256]{1,0:T(8,128)(2,1)S(1)} %constant_dynamic-slice_fusion), channel_id=1, source_target_pairs={{0,2},{1,3},{2,0},{3,1},{4,6},{5,7},{6,4},{7,5},{8,10},{9,11},{10,... | collective-permute-start | bytes 294920 | tf_op jit(solution)/shard_map/ppermute | solution.py:96
  16.9 3.1 %collective-permute-start.2 = (bf16[192,256]{1,0:T(8,128)(2,1)S(1)}, bf16[192,256]{1,0:T(8,128)(2,1)S(1)}, u32[]{:S(2)}, u32[]{:S(2)}) collective-permute-start(bf16[192,256]{1,0:T(8,128)(2,1)S(1)} %constant_dynamic-slice_fusion), channel_id=1, source_target_pairs={{0,3},{1,0},{2,1},{3,2},{4,7},{5,4},{6,5},{7,6},{8,11},{9,8},{10,9... | collective-permute-start | bytes 294920 | tf_op jit(solution)/shard_map/ppermute | solution.py:96
  20.0 2.6 %collective-permute-done.2 = bf16[192,256]{1,0:T(8,128)(2,1)S(1)} collective-permute-done((bf16[192,256]{1,0:T(8,128)(2,1)S(1)}, bf16[192,256]{1,0:T(8,128)(2,1)S(1)}, u32[]{:S(2)}, u32[]{:S(2)}) %collective-permute-start.2) | collective-permute-done | bytes 98336 | tf_op jit(solution)/shard_map/ppermute | solution.py:96
  22.6 0.8 pad_maximum_fusion.1
  23.3 0.0 all-gather.2.cloned.1.call-update
  23.4 0.7 bitcast_select_fusion
  24.1 0.6 broadcast_in_dim.11
  24.7 12.4 %all-to-all-start = ((s32[16,4,128]{2,1,0:T(4,128)}), s32[16,4,128]{2,1,0:T(4,128)S(1)}, u32[]{:S(2)}, u32[]{:S(2)}) async-start(s32[16,4,128]{2,1,0:T(4,128)} %broadcast_in_dim.11), calls=%async_computation | async-start | bytes 65536 | tf_op jit(solution)/shard_map/all_to_all | solution.py:61
  37.1 7.4 %all-to-all-done = s32[16,4,128]{2,1,0:T(4,128)S(1)} async-done(((s32[16,4,128]{2,1,0:T(4,128)}), s32[16,4,128]{2,1,0:T(4,128)S(1)}, u32[]{:S(2)}, u32[]{:S(2)}) %all-to-all-start) | async-done | bytes 32800 | tf_op jit(solution)/shard_map/all_to_all | solution.py:61
  44.5 1.4 pad_maximum_fusion
  45.9 1.5 copy.34
  47.4 4.6 %all-to-all-start.1 = ((bf16[16,256,256]{2,1,0:T(8,128)(2,1)}), bf16[16,256,256]{2,1,0:T(8,128)(2,1)}, u32[]{:S(2)}, u32[]{:S(2)}) async-start(bf16[16,256,256]{2,1,0:T(8,128)(2,1)} %bitcast.61), calls=%async_computation.1 | async-start | bytes 4194304 | tf_op jit(solution)/shard_map/all_to_all | solution.py:93
  52.0 0.0 reduce-scatter.2.cloned.1.call-start
  52.0 0.1 add_multiply_fusion
  52.1 0.1 iota_add_fusion
  52.2 0.1 slice_bitcast_fusion.1
  52.3 0.1 transpose_reshape.6.b_ref
  52.4 0.1 transpose_reshape.7.b_ref
  52.5 0.8 dynamic-slice_convert_fusion
  53.2 0.4 copy.26
  53.6 15.6 %shard_map.77 = bf16[2048,3584]{1,0:T(8,128)(2,1)S(1)} custom-call(s32[2048,4]{1,0:T(8,128)S(1)} %bitcast.59, s32[1,3584]{1,0:T(1,128)S(1)} %transpose_reshape.6.b_ref), custom_call_target="tpu_custom_call" | custom-call | flops 88080384 | bytes 14680064 | tf_op jit(solution)/shard_map/pallas_call | solution.py:39
  69.2 5.2 %copy-done.1 = bf16[2048,3584]{1,0:T(8,128)(2,1)} copy-done((bf16[2048,3584]{1,0:T(8,128)(2,1)}, bf16[2048,3584]{1,0:T(8,128)(2,1)S(1)}, u32[]{:S(2)}) %copy-start.1) | copy-done | bytes 14680088
  74.4 12.5 %shard_map.78 = bf16[2048,2560]{1,0:T(8,128)(2,1)S(1)} custom-call(s32[2048,4]{1,0:T(8,128)S(1)} %bitcast.60, s32[1,2560]{1,0:T(1,128)S(1)} %transpose_reshape.7.b_ref), custom_call_target="tpu_custom_call" | custom-call | flops 62914560 | bytes 10485760 | tf_op jit(solution)/shard_map/pallas_call | solution.py:39
  86.9 3.9 %copy-done.2 = bf16[2048,2560]{1,0:T(8,128)(2,1)} copy-done((bf16[2048,2560]{1,0:T(8,128)(2,1)}, bf16[2048,2560]{1,0:T(8,128)(2,1)S(1)}, u32[]{:S(2)}) %copy-start.2) | copy-done | bytes 10485784
  90.8 0.0 all-gather.2.cloned.1.call-done
  90.8 1.4 slice.73
  92.2 1.7 slice_bitcast_fusion
  93.9 0.1 copy.28
  94.1 7.4 %fusion.28 = f32[2048,256]{1,0:T(8,128)S(1)} fusion(bf16[2048,3584]{1,0:T(8,128)(2,1)} %copy-done.1, bf16[3584,256]{1,0:T(8,128)(2,1)S(1)} %bitcast.67), kind=kOutput, calls=%fused_computation.52 | convolution fusion | flops 3758096384 | bytes 18612224 | tf_op jit(solution)/shard_map/dot_general | solution.py:111
  101.5 0.1 slice-done.1
  101.6 0.6 slice-done.2
  102.2 4.4 %convolution_add_fusion = f32[2048,256]{1,0:T(8,128)} fusion(f32[2048,256]{1,0:T(8,128)S(1)} %fusion.28, bf16[2048,2560]{1,0:T(8,128)(2,1)S(1)} %bitcast.58, bf16[2560,256]{1,0:T(8,128)(2,1)S(1)} %bitcast.68), kind=kOutput, calls=%fused_computation.8 | convolution fusion | flops 2684878848 | bytes 15990784 | tf_op jit(solution)/shard_map/dot_general | solution.py:112
  106.6 1.9 fusion.26
  108.5 0.3 copy-done.3
  108.9 2.0 multiply_reduce_fusion
  110.9 18.8 %all_to_all.25 = f32[16,32,128]{2,1,0:T(8,128)S(1)} all-to-all(f32[16,32,128]{2,1,0:T(8,128)S(1)} %broadcast_in_dim.13), channel_id=1, replica_groups=mesh['z'=8,'c'=2,'y'=8,'x'=4] {'z','c'}, dimensions={0} | all-to-all | bytes 524288 | tf_op jit(solution)/shard_map/all_to_all | solution.py:61
  129.8 4.2 %multiply_convert_fusion = (bf16[2048,256]{1,0:T(8,128)(2,1)}, bf16[2048,256]{1,0:T(8,128)(2,1)S(1)}) fusion(f32[2048,256]{1,0:T(8,128)} %get-tuple-element.40, f32[2048]{0:T(1024)S(1)} %get-tuple-element.48, f32[256]{0:T(256)S(1)} %dynamic-slice_convert_fusion, f32[2048]{0:T(1024)S(1)} %bitcast.72, f32[2048]{0:T(1024)S(1)} %get-tuple-element.49, ...), kind=kLoop, calls=%fused_computation.18 | loop fusion | flops 5767168 | bytes 5276672 | tf_op jit(solution)/shard_map/convert_element_type | solution.py:123
  133.9 0.9 copy-done.5
  134.9 8.5 %fusion.29 = f32[2560,256]{1,0:T(8,128)} fusion(bf16[2048,2560]{1,0:T(8,128)(2,1)} %copy-done.2, bf16[2048,256]{1,0:T(8,128)(2,1)S(1)} %get-tuple-element.30), kind=kOutput, calls=%fused_computation.53 | convolution fusion | flops 2684354560 | bytes 14155776 | tf_op jit(solution)/shard_map/dot_general | solution.py:70
  143.4 3.7 %all-to-all-start.3 = ((bf16[16,128,256]{2,1,0:T(8,128)(2,1)}), bf16[16,128,256]{2,1,0:T(8,128)(2,1)S(1)}, u32[]{:S(2)}, u32[]{:S(2)}) async-start(bf16[16,128,256]{2,1,0:T(8,128)(2,1)} %bitcast.64), calls=%async_computation.3 | async-start | bytes 2097152 | tf_op jit(solution)/shard_map/all_to_all | solution.py:143
  147.1 3.6 %fusion.20 = bf16[896,256]{1,0:T(8,128)(2,1)S(1)} fusion(bf16[2048,256]{1,0:T(8,128)(2,1)} %copy-done.5, bf16[2048,3584]{1,0:T(8,128)(2,1)} %copy-done.1), kind=kOutput, calls=%fused_computation.24 | convolution fusion | flops 939753472 | bytes 5177344 | tf_op jit(solution)/shard_map/dot_general | solution.py:70
  150.7 3.2 %fusion.17 = bf16[896,256]{1,0:T(8,128)(2,1)S(1)} fusion(bf16[2048,256]{1,0:T(8,128)(2,1)S(1)} %copy-done.6, bf16[2048,3584]{1,0:T(8,128)(2,1)} %copy-done.1), kind=kOutput, calls=%fused_computation.23 | convolution fusion | flops 939753472 | bytes 5177344 | tf_op jit(solution)/shard_map/dot_general | solution.py:70
  154.0 3.3 %fusion.14 = bf16[896,256]{1,0:T(8,128)(2,1)S(1)} fusion(bf16[2048,256]{1,0:T(8,128)(2,1)S(1)} %copy-done.6, bf16[2048,3584]{1,0:T(8,128)(2,1)} %copy-done.1), kind=kOutput, calls=%fused_computation.22 | convolution fusion | flops 939753472 | bytes 5177344 | tf_op jit(solution)/shard_map/dot_general | solution.py:70
  157.2 2.1 collective-permute-start.3
  159.3 4.4 %collective-permute-start.4 = (bf16[896,256]{1,0:T(8,128)(2,1)S(1)}, bf16[896,256]{1,0:T(8,128)(2,1)S(1)}, u32[]{:S(2)}, u32[]{:S(2)}) collective-permute-start(bf16[896,256]{1,0:T(8,128)(2,1)S(1)} %fusion.17), channel_id=1, source_target_pairs={{0,3},{1,0},{2,1},{3,2},{4,7},{5,4},{6,5},{7,6},{8,11},{9,8},{10,9... | collective-permute-start | bytes 1376264 | tf_op jit(solution)/shard_map/ppermute | solution.py:139
  163.7 2.8 %collective-permute-start.5 = (bf16[896,256]{1,0:T(8,128)(2,1)S(1)}, bf16[896,256]{1,0:T(8,128)(2,1)S(1)}, u32[]{:S(2)}, u32[]{:S(2)}) collective-permute-start(bf16[896,256]{1,0:T(8,128)(2,1)S(1)} %fusion.20), channel_id=1, source_target_pairs={{0,2},{1,3},{2,0},{3,1},{4,6},{5,7},{6,4},{7,5},{8,10},{9,11},{10,... | collective-permute-start | bytes 1376264 | tf_op jit(solution)/shard_map/ppermute | solution.py:139
  166.5 3.2 %fusion.6 = f32[896,256]{1,0:T(8,128)S(1)} fusion(bf16[2048,256]{1,0:T(8,128)(2,1)S(1)} %copy-done.6, bf16[2048,3584]{1,0:T(8,128)(2,1)} %copy-done.1), kind=kOutput, calls=%fused_computation.6 | convolution fusion | flops 939524096 | bytes 5636096 | tf_op jit(solution)/shard_map/dot_general | solution.py:70
  169.8 3.0 %collective-permute-done.3 = bf16[896,256]{1,0:T(8,128)(2,1)S(1)} collective-permute-done((bf16[896,256]{1,0:T(8,128)(2,1)S(1)}, bf16[896,256]{1,0:T(8,128)(2,1)S(1)}, u32[]{:S(2)}, u32[]{:S(2)}) %collective-permute-start.3) | collective-permute-done | bytes 458784 | tf_op jit(solution)/shard_map/ppermute | solution.py:139
  172.8 10.6 %collective-permute-done.4 = bf16[896,256]{1,0:T(8,128)(2,1)S(1)} collective-permute-done((bf16[896,256]{1,0:T(8,128)(2,1)S(1)}, bf16[896,256]{1,0:T(8,128)(2,1)S(1)}, u32[]{:S(2)}, u32[]{:S(2)}) %collective-permute-start.4) | collective-permute-done | bytes 458784 | tf_op jit(solution)/shard_map/ppermute | solution.py:139
  183.4 1.0 add_convert_fusion
  184.4 6.8 %all-to-all-start.4 = ((bf16[8,112,256]{2,1,0:T(8,128)(2,1)}), bf16[8,112,256]{2,1,0:T(8,128)(2,1)S(1)}, u32[]{:S(2)}, u32[]{:S(2)}) async-start(bf16[8,112,256]{2,1,0:T(8,128)(2,1)} %bitcast.16), calls=%async_computation.5 | async-start | bytes 917504 | tf_op jit(solution)/shard_map/all_to_all | solution.py:149
  191.1 1.1 copy.32
  192.2 1.0 fusion.27
  193.2 5.4 %collective-permute-start.6 = (f32[80,256]{1,0:T(8,128)S(1)}, f32[80,256]{1,0:T(8,128)S(1)}, u32[]{:S(2)}, u32[]{:S(2)}) collective-permute-start(f32[80,256]{1,0:T(8,128)S(1)} %get-tuple-element.47), channel_id=1, source_target_pairs={{0,3},{1,0},{2,1},{3,2},{4,7},{5,4},{6,5},{7,6},{8,11},{9,8},{10,9... | collective-permute-start | bytes 245768 | tf_op jit(solution)/shard_map/ppermute | solution.py:152
  198.6 2.7 %collective-permute-start.7 = (f32[80,256]{1,0:T(8,128)S(1)}, f32[80,256]{1,0:T(8,128)S(1)}, u32[]{:S(2)}, u32[]{:S(2)}) collective-permute-start(f32[80,256]{1,0:T(8,128)S(1)} %get-tuple-element.45), channel_id=1, source_target_pairs={{0,2},{1,3},{2,0},{3,1},{4,6},{5,7},{6,4},{7,5},{8,10},{9,11},{10,... | collective-permute-start | bytes 245768 | tf_op jit(solution)/shard_map/ppermute | solution.py:152
  201.4 1.9 collective-permute-start.8
  203.3 3.0 %all-to-all-done.4 = bf16[8,112,256]{2,1,0:T(8,128)(2,1)S(1)} async-done(((bf16[8,112,256]{2,1,0:T(8,128)(2,1)}), bf16[8,112,256]{2,1,0:T(8,128)(2,1)S(1)}, u32[]{:S(2)}, u32[]{:S(2)}) %all-to-all-start.4) | async-done | bytes 458784 | tf_op jit(solution)/shard_map/all_to_all | solution.py:149
  206.3 0.1 convert_reduce_fusion
  206.4 1.9 collective-permute-done.8
  208.3 0.9 slice_add_fusion
  209.2 0.7 pad_maximum_fusion.2
  (36 shorter events, 0.2 us)
Async XLA Ops:
  7.2 1.4 copy-start
  7.2 37.3 %copy-start.4 = (bf16[128,4096]{1,0:T(8,128)(2,1)S(1)}, bf16[128,4096]{1,0:T(8,128)(2,1)}, u32[]{:S(2)}) copy-start(bf16[128,4096]{1,0:T(8,128)(2,1)} %param.11) | copy-start | bytes 3145732
  7.2 83.6 %all-gather.2.cloned.1.call-start = ((), (), s32[]{:S(2)}) async-start(), calls=%async_computation.6 | async-start | bytes 3538944 | tf_op jit(solution)/shard_map/all_gather | solution.py:97
  8.6 11.4 %collective-permute-start = (bf16[192,256]{1,0:T(8,128)(2,1)S(1)}, bf16[192,256]{1,0:T(8,128)(2,1)S(1)}, u32[]{:S(2)}, u32[]{:S(2)}) collective-permute-start(bf16[192,256]{1,0:T(8,128)(2,1)S(1)} %constant_dynamic-slice_fusion), channel_id=1, source_target_pairs={{0,1},{1,2},{2,3},{3,0},{4,5},{5,6},{6,7},{7,4},{8,9},{9,10},{10,1... | collective-permute-start | bytes 294920 | tf_op jit(solution)/shard_map/ppermute | solution.py:96
  12.6 7.4 %collective-permute-start.1 = (bf16[192,256]{1,0:T(8,128)(2,1)S(1)}, bf16[192,256]{1,0:T(8,128)(2,1)S(1)}, u32[]{:S(2)}, u32[]{:S(2)}) collective-permute-start(bf16[192,256]{1,0:T(8,128)(2,1)S(1)} %constant_dynamic-slice_fusion), channel_id=1, source_target_pairs={{0,2},{1,3},{2,0},{3,1},{4,6},{5,7},{6,4},{7,5},{8,10},{9,11},{10,... | collective-permute-start | bytes 294920 | tf_op jit(solution)/shard_map/ppermute | solution.py:96
  16.9 5.7 %collective-permute-start.2 = (bf16[192,256]{1,0:T(8,128)(2,1)S(1)}, bf16[192,256]{1,0:T(8,128)(2,1)S(1)}, u32[]{:S(2)}, u32[]{:S(2)}) collective-permute-start(bf16[192,256]{1,0:T(8,128)(2,1)S(1)} %constant_dynamic-slice_fusion), channel_id=1, source_target_pairs={{0,3},{1,0},{2,1},{3,2},{4,7},{5,4},{6,5},{7,6},{8,11},{9,8},{10,9... | collective-permute-start | bytes 294920 | tf_op jit(solution)/shard_map/ppermute | solution.py:96
  24.7 19.8 %all-to-all-start = ((s32[16,4,128]{2,1,0:T(4,128)}), s32[16,4,128]{2,1,0:T(4,128)S(1)}, u32[]{:S(2)}, u32[]{:S(2)}) async-start(s32[16,4,128]{2,1,0:T(4,128)} %broadcast_in_dim.11), calls=%async_computation | async-start | bytes 65536 | tf_op jit(solution)/shard_map/all_to_all | solution.py:61
  47.4 59.2 %all-to-all-start.1 = ((bf16[16,256,256]{2,1,0:T(8,128)(2,1)}), bf16[16,256,256]{2,1,0:T(8,128)(2,1)}, u32[]{:S(2)}, u32[]{:S(2)}) async-start(bf16[16,256,256]{2,1,0:T(8,128)(2,1)} %bitcast.61), calls=%async_computation.1 | async-start | bytes 4194304 | tf_op jit(solution)/shard_map/all_to_all | solution.py:93
  52.0 140.2 %reduce-scatter.2.cloned.1.call-start = ((), (), s32[]{:S(2)}) async-start(), calls=%async_computation.7 | async-start | bytes 2949120 | tf_op jit(solution)/shard_map/reduce_scatter | solution.py:129
  69.2 5.2 %copy-start.1 = (bf16[2048,3584]{1,0:T(8,128)(2,1)}, bf16[2048,3584]{1,0:T(8,128)(2,1)S(1)}, u32[]{:S(2)}) copy-start(bf16[2048,3584]{1,0:T(8,128)(2,1)S(1)} %shard_map.77) | copy-start | bytes 44040196
  86.9 3.9 %copy-start.2 = (bf16[2048,2560]{1,0:T(8,128)(2,1)}, bf16[2048,2560]{1,0:T(8,128)(2,1)S(1)}, u32[]{:S(2)}) copy-start(bf16[2048,2560]{1,0:T(8,128)(2,1)S(1)} %shard_map.78) | copy-start | bytes 31457284
  93.9 7.6 %slice-start = ((s8[10485760]{0:T(1024)(128)(4,1)}), s8[4194304]{0:T(1024)(128)(4,1)S(1)}, s32[]{:S(2)}) async-start(s8[10485760]{0:T(1024)(128)(4,1)} %bitcast.57), calls=%async_computation.8 | async-start | bytes 8388608
  94.1 7.5 %slice-start.1 = ((s8[10485760]{0:T(1024)(128)(4,1)}), s8[4194304]{0:T(1024)(128)(4,1)S(1)}, s32[]{:S(2)}) async-start(s8[10485760]{0:T(1024)(128)(4,1)} %bitcast.57), calls=%async_computation.9 | async-start | bytes 8388608
  94.1 8.1 %slice-start.2 = ((s8[10485760]{0:T(1024)(128)(4,1)}), s8[2097152]{0:T(1024)(128)(4,1)S(1)}, s32[]{:S(2)}) async-start(s8[10485760]{0:T(1024)(128)(4,1)} %bitcast.57), calls=%async_computation.10 | async-start | bytes 4194304
  106.6 2.2 %copy-start.3 = (f32[2048,256]{1,0:T(8,128)S(1)}, f32[2048,256]{1,0:T(8,128)}, u32[]{:S(2)}) copy-start(f32[2048,256]{1,0:T(8,128)} %convolution_add_fusion) | copy-start | bytes 6291460
  133.9 1.0 copy-start.5
  143.4 41.0 %all-to-all-start.3 = ((bf16[16,128,256]{2,1,0:T(8,128)(2,1)}), bf16[16,128,256]{2,1,0:T(8,128)(2,1)S(1)}, u32[]{:S(2)}, u32[]{:S(2)}) async-start(bf16[16,128,256]{2,1,0:T(8,128)(2,1)} %bitcast.64), calls=%async_computation.3 | async-start | bytes 2097152 | tf_op jit(solution)/shard_map/all_to_all | solution.py:143
  147.1 3.6 %copy-start.6 = (bf16[2048,256]{1,0:T(8,128)(2,1)S(1)}, bf16[2048,256]{1,0:T(8,128)(2,1)}, u32[]{:S(2)}) copy-start(bf16[2048,256]{1,0:T(8,128)(2,1)} %copy-done.5) | copy-start | bytes 3145732
  157.2 15.6 %collective-permute-start.3 = (bf16[896,256]{1,0:T(8,128)(2,1)S(1)}, bf16[896,256]{1,0:T(8,128)(2,1)S(1)}, u32[]{:S(2)}, u32[]{:S(2)}) collective-permute-start(bf16[896,256]{1,0:T(8,128)(2,1)S(1)} %fusion.14), channel_id=1, source_target_pairs={{0,1},{1,2},{2,3},{3,0},{4,5},{5,6},{6,7},{7,4},{8,9},{9,10},{10,1... | collective-permute-start | bytes 1376264 | tf_op jit(solution)/shard_map/ppermute | solution.py:139
  159.3 24.0 %collective-permute-start.4 = (bf16[896,256]{1,0:T(8,128)(2,1)S(1)}, bf16[896,256]{1,0:T(8,128)(2,1)S(1)}, u32[]{:S(2)}, u32[]{:S(2)}) collective-permute-start(bf16[896,256]{1,0:T(8,128)(2,1)S(1)} %fusion.17), channel_id=1, source_target_pairs={{0,3},{1,0},{2,1},{3,2},{4,7},{5,4},{6,5},{7,6},{8,11},{9,8},{10,9... | collective-permute-start | bytes 1376264 | tf_op jit(solution)/shard_map/ppermute | solution.py:139
  163.7 19.6 %collective-permute-start.5 = (bf16[896,256]{1,0:T(8,128)(2,1)S(1)}, bf16[896,256]{1,0:T(8,128)(2,1)S(1)}, u32[]{:S(2)}, u32[]{:S(2)}) collective-permute-start(bf16[896,256]{1,0:T(8,128)(2,1)S(1)} %fusion.20), channel_id=1, source_target_pairs={{0,2},{1,3},{2,0},{3,1},{4,6},{5,7},{6,4},{7,5},{8,10},{9,11},{10,... | collective-permute-start | bytes 1376264 | tf_op jit(solution)/shard_map/ppermute | solution.py:139
  184.4 22.0 %all-to-all-start.4 = ((bf16[8,112,256]{2,1,0:T(8,128)(2,1)}), bf16[8,112,256]{2,1,0:T(8,128)(2,1)S(1)}, u32[]{:S(2)}, u32[]{:S(2)}) async-start(bf16[8,112,256]{2,1,0:T(8,128)(2,1)} %bitcast.16), calls=%async_computation.5 | async-start | bytes 917504 | tf_op jit(solution)/shard_map/all_to_all | solution.py:149
  193.2 13.2 %collective-permute-start.6 = (f32[80,256]{1,0:T(8,128)S(1)}, f32[80,256]{1,0:T(8,128)S(1)}, u32[]{:S(2)}, u32[]{:S(2)}) collective-permute-start(f32[80,256]{1,0:T(8,128)S(1)} %get-tuple-element.47), channel_id=1, source_target_pairs={{0,3},{1,0},{2,1},{3,2},{4,7},{5,4},{6,5},{7,6},{8,11},{9,8},{10,9... | collective-permute-start | bytes 245768 | tf_op jit(solution)/shard_map/ppermute | solution.py:152
  198.6 7.8 %collective-permute-start.7 = (f32[80,256]{1,0:T(8,128)S(1)}, f32[80,256]{1,0:T(8,128)S(1)}, u32[]{:S(2)}, u32[]{:S(2)}) collective-permute-start(f32[80,256]{1,0:T(8,128)S(1)} %get-tuple-element.45), channel_id=1, source_target_pairs={{0,2},{1,3},{2,0},{3,1},{4,6},{5,7},{6,4},{7,5},{8,10},{9,11},{10,... | collective-permute-start | bytes 245768 | tf_op jit(solution)/shard_map/ppermute | solution.py:152
  201.4 6.9 %collective-permute-start.8 = (f32[80,256]{1,0:T(8,128)S(1)}, f32[80,256]{1,0:T(8,128)S(1)}, u32[]{:S(2)}, u32[]{:S(2)}) collective-permute-start(f32[80,256]{1,0:T(8,128)S(1)} %get-tuple-element.46), channel_id=1, source_target_pairs={{0,1},{1,2},{2,3},{3,0},{4,5},{5,6},{6,7},{7,4},{8,9},{9,10},{10,1... | collective-permute-start | bytes 245768 | tf_op jit(solution)/shard_map/ppermute | solution.py:152
Sparse Core Ops, SparseCore 0:
  23.5 52.4 all-gather.1
  143.5 38.7 reduce-scatter.1

commit v3 on v2

v3 whole, which is shorter than its diff:
```python
import functools

import jax
import jax.numpy as jnp
from jax import lax
from jax.experimental import pallas as pl
from jax.experimental.pallas import tpu as pltpu
from jax.sharding import Mesh, PartitionSpec as P

Z, C, Y, X = 8, 2, 8, 4
G = ("z", "c")
T = ("y", "x")
ROWS_Y = 80


def count_kernel(step, wide, a_ref, b_ref, out_ref):
    rows, cols = out_ref.shape
    one = jnp.ones((step, wide), jnp.bfloat16)
    zero = jnp.zeros((step, wide), jnp.bfloat16)

    def strip(i, carry):
        here = pl.ds(pl.multiple_of(i * step, step), step)
        a = a_ref[here, :]
        a = [
            jnp.broadcast_to(a[:, k : k + 1], (step, wide)).astype(jnp.int16)
            for k in range(a.shape[1])
        ]
        for j in range(0, cols, wide):
            b = b_ref[:, j : j + wide]
            terms = [jnp.where(ak == b, one, zero) for ak in a]
            out_ref[here, j : j + wide] = (terms[0] + terms[1]) + (terms[2] + terms[3])
        return carry

    lax.fori_loop(0, rows // step, strip, 0)


def count_matrix(a, b, block):
    rows, cols, step = a.shape[0], b.shape[0], 32
    b = jnp.broadcast_to(b.astype(jnp.int16)[None, :], (step, cols))
    return pl.pallas_call(
        functools.partial(count_kernel, step, 256),
        grid=(rows // block,),
        in_specs=[
            pl.BlockSpec((block, a.shape[1]), lambda i: (i, 0)),
            pl.BlockSpec(b.shape, lambda i: (0, 0)),
        ],
        out_specs=pl.BlockSpec((block, cols), lambda i: (i, 0)),
        out_shape=jax.ShapeDtypeStruct((rows, cols), jnp.bfloat16),
        cost_estimate=pl.CostEstimate(
            flops=rows * cols * 12, bytes_accessed=rows * cols * 2, transcendentals=0
        ),
        compiler_params=pltpu.CompilerParams(vmem_limit_bytes=60 * 2**20),
    )(a, b)


def pool_kernel(hot_ref, table_ref, out_ref):
    out_ref[...] = jnp.dot(hot_ref[...], table_ref[...], preferred_element_type=jnp.float32)


def pool(hot, table, block):
    tok, span = hot.shape
    width = table.shape[1]
    return pl.pallas_call(
        pool_kernel,
        grid=(tok // block,),
        in_specs=[
            pl.BlockSpec((block, span), lambda i: (i, 0)),
            pl.BlockSpec((span, width), lambda i: (0, 0)),
        ],
        out_specs=pl.BlockSpec((block, width), lambda i: (i, 0)),
        out_shape=jax.ShapeDtypeStruct((tok, width), jnp.float32),
        cost_estimate=pl.CostEstimate(
            flops=2 * tok * width * span,
            bytes_accessed=2 * (tok + width) * span + 4 * tok * width,
            transcendentals=0,
        ),
        compiler_params=pltpu.CompilerParams(vmem_limit_bytes=60 * 2**20),
    )(hot, table)


def rows_kernel(hot_ref, grad_ref, by_y_ref, *by_x_refs):
    out = lax.dot_general(
        hot_ref[...],
        grad_ref[...],
        (((0,), (0,)), ((), ())),
        preferred_element_type=jnp.float32,
    )
    out = out.reshape(X, out.shape[0] // X, out.shape[1])
    by_y_ref[0] = out[:, :ROWS_Y]
    for s, ref in enumerate(by_x_refs):
        ref[0] = out[s, ROWS_Y:].astype(ref.dtype)


def rows_of(hot, token_grad, rows):
    tok, width = token_grad.shape
    span = hot.shape[1]
    late = rows - ROWS_Y
    return pl.pallas_call(
        rows_kernel,
        grid=(Y,),
        in_specs=[
            pl.BlockSpec((tok, span // Y), lambda i: (0, i)),
            pl.BlockSpec((tok, width), lambda i: (0, 0)),
        ],
        out_specs=[pl.BlockSpec((1, X, ROWS_Y, width), lambda i: (i, 0, 0, 0))]
        + [pl.BlockSpec((1, late, width), lambda i: (i, 0, 0))] * X,
        out_shape=[jax.ShapeDtypeStruct((Y, X, ROWS_Y, width), jnp.float32)]
        + [
            jax.ShapeDtypeStruct((Y, late, width), jnp.bfloat16 if s else jnp.float32)
            for s in range(X)
        ],
        cost_estimate=pl.CostEstimate(
            flops=2 * tok * width * span,
            bytes_accessed=2 * tok * (span + width) + 4 * span * width,
            transcendentals=0,
        ),
        compiler_params=pltpu.CompilerParams(vmem_limit_bytes=60 * 2**20),
    )(hot, token_grad)


def shift(s):
    return [(i, (i + s) % X) for i in range(X)]


def spread(v, n, axis):
    whole = jnp.broadcast_to(v[None], (n,) + v.shape)
    return lax.all_to_all(whole, axis, split_axis=0, concat_axis=0, tiled=True)


def per_device(embedded, ngram_ids, counts, slab, gain, cotangent):
    tok, features = embedded.shape
    ngram = ngram_ids.shape[1]
    rows = slab.shape[0]
    blocks = Z * C
    width = features // blocks
    all_rows = rows * Y * X
    all_tok = tok * blocks
    mine = lax.axis_index(G) * width
    here_x = lax.axis_index("x")

    ids = jnp.where(jnp.arange(ngram)[:, None] < counts[None, :], ngram_ids.T, -1)
    ids = spread(ids, blocks, G)

    sent = jnp.concatenate([embedded, cotangent], axis=0)
    sent = sent.reshape(2 * tok, blocks, width).transpose(1, 0, 2)
    ids, sent = lax.optimization_barrier((ids, sent))
    came = lax.all_to_all(sent, G, split_axis=0, concat_axis=0, tiled=True)
    ids = ids.transpose(0, 2, 1).reshape(all_tok, ngram)

    piece = lax.dynamic_slice(slab, (0, mine), (rows, width))
    pieces = [piece] + [lax.ppermute(piece, "x", shift(s)) for s in range(1, X)]
    table = lax.all_gather(jnp.concatenate(pieces, axis=0), "y", tiled=True)
    owner = jnp.arange(Y)[:, None] * X + (here_x - jnp.arange(X)) % X
    table_row = (owner[:, :, None] * rows + jnp.arange(rows)).reshape(all_rows)

    count_f = jnp.sum((ids >= 0).astype(jnp.float32), axis=1, keepdims=True)
    hot = count_matrix(ids, table_row, 256)

    gain_f = lax.dynamic_slice(gain, (mine,), (width,)).astype(jnp.float32)

    pooled = pool(hot, table, 256)
    pooled, came = lax.optimization_barrier((pooled, came))
    emb = came[:, :tok].reshape(all_tok, width).astype(jnp.float32)
    cot = came[:, tok:].reshape(all_tok, width).astype(jnp.float32)
    hidden = emb + pooled / count_f
    grad_out = cot * gain_f
    sums = jnp.stack([jnp.sum(hidden * hidden, axis=1), jnp.sum(hidden * grad_out, axis=1)])
    sums = spread(sums.reshape(2 * all_tok // 128, 128), blocks, G)
    sums = jnp.sum(sums.reshape(blocks, 2, all_tok), axis=0) / features
    inv_rms = lax.rsqrt(sums[0] + 1e-05)[:, None]
    inner = sums[1][:, None]
    normed = (hidden * inv_rms * gain_f).astype(jnp.bfloat16)
    grad_hidden = inv_rms * grad_out - hidden * (inv_rms * inv_rms * inv_rms) * inner
    token_grad = lax.optimization_barrier((grad_hidden / count_f).astype(jnp.bfloat16))

    by_y, *by_x = rows_of(hot, token_grad, rows)
    by_y = lax.psum_scatter(
        by_y.reshape(Y * X * ROWS_Y, width), "y", scatter_dimension=0, tiled=True
    )
    by_x = [by_x[0]] + [lax.ppermute(by_x[s], "x", shift(-s)) for s in (2, 1, 3)]
    by_x = sum(v.astype(jnp.float32) for v in by_x).astype(jnp.bfloat16)

    back = lax.all_to_all(
        normed.reshape(blocks, tok, width), G, split_axis=0, concat_axis=0, tiled=True
    )

    by_x, back = lax.optimization_barrier((by_x, back))
    normed = back.transpose(1, 0, 2).reshape(tok, features)
    by_x = lax.all_to_all(by_x, "y", split_axis=0, concat_axis=0, tiled=True)
    by_x = jnp.sum(by_x.astype(jnp.float32), axis=0)
    by_y = by_y.reshape(X, ROWS_Y, width)
    by_y = by_y[0] + sum(lax.ppermute(by_y[s], "x", shift(-s)) for s in range(1, X))
    row_grads = jnp.concatenate([by_y, by_x], axis=0)
    return (normed, row_grads)


def solution(mesh):
    fine = Mesh(mesh.devices.reshape(Z, C, Y, X), ("z", "c", "y", "x"))
    every = ("z", "c", "y", "x")
    in_specs = (P(every, None), P(every, None), P(every), P(T, None), P(), P(every, None))
    out_specs = (P(every, None), P(T, G))
    return jax.shard_map(
        per_device, mesh=fine, in_specs=in_specs, out_specs=out_specs, check_vma=False
    )
```

time: 219 us -> 207 us (0.945)
  the two profiles are of different devices: /device:TPU:1 before, /device:TPU:30 now
where the time goes in v3:
time: 207 us; the launch traced here: 206 us
  starting transfers between devices  56.3 us (27%)
  waiting for transfers between devices  48.7 us (24%)
  Pallas kernels  48.2 us (23%)
  blocking collectives  15.7 us (8%)
  between operations  14.3 us (7%)
  other arithmetic  12.9 us (6%)
  local copies, waits for them, and re-layouts  10 us (5%)
    pallas_call x1, Pallas kernels, count_matrix(): pl.pallas_call(functools.partial(count_kernel, step, 256), grid=(rows //...  18.3 us
    ppermute x3, waiting for transfers between devices, per_device(): lax.ppermute(by_x[s], 'x', shift(-s))  16 us
    all_to_all x1, blocking collectives, spread(): return lax.all_to_all(whole, axis, split_axis=0, concat_axis=0, tiled=True)  15.7 us
    pallas_call x1, Pallas kernels, pool(): pl.pallas_call(pool_kernel, grid=(tok // block,), in_specs=[pl.BlockSpec(...  15.1 us
    pallas_call x1, Pallas kernels, rows_of(): pl.pallas_call(rows_kernel, grid=(Y,), in_specs=[pl.BlockSpec((tok, span...  14.9 us
    ppermute x3, starting transfers between devices, per_device(): lax.ppermute(by_x[s], 'x', shift(-s))  11.1 us
    all_to_all x1, starting transfers between devices, spread(): return lax.all_to_all(whole, axis, split_axis=0, concat_axis=0, tiled=True)  10.4 us
    ppermute x3, starting transfers between devices, per_device(): pieces = [piece] + [lax.ppermute(piece, 'x', shift(s)) for s in range(1, X)]  9.76 us
  transfers between devices with their start and end apart: 15, of which 10 were waited for; matrix products, arithmetic and copies ran while one was open for 5% of the time, Pallas kernels for 16%

profile of v3, /device:TPU:30, one launch (start us, length us, event | category | flops | bytes accessed | tf_op | source)
XLA Modules:
  0.0 206.0 jit_solution(571750987283173837)
XLA Ops:
  7.2 0.0 copy-start
  7.2 0.0 copy-start.2
  7.2 0.0 all-gather.2.cloned.1.call-start
  7.2 1.3 copy-done
  8.6 2.7 %collective-permute-start.2 = (bf16[192,256]{1,0:T(8,128)(2,1)S(1)}, bf16[192,256]{1,0:T(8,128)(2,1)S(1)}, u32[]{:S(2)}, u32[]{:S(2)}) collective-permute-start(bf16[192,256]{1,0:T(8,128)(2,1)S(1)} %constant_dynamic-slice_fusion), channel_id=1, source_target_pairs={{0,3},{1,0},{2,1},{3,2},{4,7},{5,4},{6,5},{7,6},{8,11},{9,8},{10,9... | collective-permute-start | bytes 294920 | tf_op jit(solution)/shard_map/ppermute | solution.py:151
  11.3 3.0 %collective-permute-start.1 = (bf16[192,256]{1,0:T(8,128)(2,1)S(1)}, bf16[192,256]{1,0:T(8,128)(2,1)S(1)}, u32[]{:S(2)}, u32[]{:S(2)}) collective-permute-start(bf16[192,256]{1,0:T(8,128)(2,1)S(1)} %constant_dynamic-slice_fusion), channel_id=1, source_target_pairs={{0,2},{1,3},{2,0},{3,1},{4,6},{5,7},{6,4},{7,5},{8,10},{9,11},{10,... | collective-permute-start | bytes 294920 | tf_op jit(solution)/shard_map/ppermute | solution.py:151
  14.4 4.0 %collective-permute-start = (bf16[192,256]{1,0:T(8,128)(2,1)S(1)}, bf16[192,256]{1,0:T(8,128)(2,1)S(1)}, u32[]{:S(2)}, u32[]{:S(2)}) collective-permute-start(bf16[192,256]{1,0:T(8,128)(2,1)S(1)} %constant_dynamic-slice_fusion), channel_id=1, source_target_pairs={{0,1},{1,2},{2,3},{3,0},{4,5},{5,6},{6,7},{7,4},{8,9},{9,10},{10,1... | collective-permute-start | bytes 294920 | tf_op jit(solution)/shard_map/ppermute | solution.py:151
  18.4 0.0 collective-permute-done.2
  18.4 1.0 collective-permute-done.1
  19.4 1.8 collective-permute-done
  21.2 0.8 pad_maximum_fusion.1
  22.0 0.0 all-gather.2.cloned.1.call-update
  22.0 0.7 bitcast_select_fusion
  22.7 0.6 broadcast_in_dim.13
  23.3 10.4 %all-to-all-start = ((s32[16,4,128]{2,1,0:T(4,128)}), s32[16,4,128]{2,1,0:T(4,128)S(1)}, u32[]{:S(2)}, u32[]{:S(2)}) async-start(s32[16,4,128]{2,1,0:T(4,128)} %broadcast_in_dim.13), calls=%async_computation | async-start | bytes 65536 | tf_op jit(solution)/shard_map/all_to_all | solution.py:127
  33.7 0.0 copy-done.2
  33.7 1.4 pad_maximum_fusion
  35.1 1.5 copy.20
  36.7 4.8 %all-to-all-done = s32[16,4,128]{2,1,0:T(4,128)S(1)} async-done(((s32[16,4,128]{2,1,0:T(4,128)}), s32[16,4,128]{2,1,0:T(4,128)S(1)}, u32[]{:S(2)}, u32[]{:S(2)}) %all-to-all-start) | async-done | bytes 32800 | tf_op jit(solution)/shard_map/all_to_all | solution.py:127
  41.4 4.4 %all-to-all-start.1 = ((bf16[16,256,256]{2,1,0:T(8,128)(2,1)}), bf16[16,256,256]{2,1,0:T(8,128)(2,1)}, u32[]{:S(2)}, u32[]{:S(2)}) async-start(bf16[16,256,256]{2,1,0:T(8,128)(2,1)} %bitcast.34), calls=%async_computation.1 | async-start | bytes 4194304 | tf_op jit(solution)/shard_map/all_to_all | solution.py:147
  45.9 0.0 reduce-scatter.2.cloned.1.call-start
  45.9 0.1 add_multiply_fusion
  46.0 0.1 add_convert_fusion.1
  46.1 0.1 convert_element_type.51
  46.2 0.8 dynamic-slice_convert_fusion
  47.0 1.3 copy.15
  48.3 0.8 broadcast_in_dim.14.b_ref
  49.1 18.3 %shard_map.77.hot_ref = bf16[2048,6144]{1,0:T(8,128)(2,1)} custom-call(s32[2048,4]{1,0:T(8,128)} %bitcast.36, s16[32,6144]{1,0:T(8,128)(2,1)} %broadcast_in_dim.14.b_ref), custom_call_target="tpu_custom_call" | custom-call | flops 150994944 | bytes 25165824 | tf_op jit(solution)/shard_map/pallas_call | solution.py:40
  67.4 7.2 %all-gather.2.cloned.1.call-done.table_ref = bf16[6144,256]{1,0:T(8,128)(2,1)} async-done(((bf16[768,256]{1,0:T(8,128)(2,1)}), bf16[6144,256]{1,0:T(8,128)(2,1)}) %all-gather.2.cloned.1.call-update) | async-done | bytes 3145744 | tf_op jit(solution)/shard_map/all_gather | solution.py:152
  74.6 15.1 %shard_map.78 = f32[2048,256]{1,0:T(8,128)} custom-call(bf16[2048,6144]{1,0:T(8,128)(2,1)} %shard_map.77.hot_ref, bf16[6144,256]{1,0:T(8,128)(2,1)} %all-gather.2.cloned.1.call-done.table_ref), custom_call_target="tpu_custom_call" | custom-call | flops 6442450944 | bytes 30408704 | tf_op jit(solution)/shard_map/pallas_call | solution.py:63
  89.7 5.4 %all-to-all-done.1 = bf16[16,256,256]{2,1,0:T(8,128)(2,1)} async-done(((bf16[16,256,256]{2,1,0:T(8,128)(2,1)}), bf16[16,256,256]{2,1,0:T(8,128)(2,1)}, u32[]{:S(2)}, u32[]{:S(2)}) %all-to-all-start.1) | async-done | bytes 2097184 | tf_op jit(solution)/shard_map/all_to_all | solution.py:147
  95.1 0.0 copy-start.1
  95.1 1.9 fusion.9
  96.9 0.3 copy-done.1
  97.3 2.0 multiply_reduce_fusion
  99.3 15.7 %all_to_all.25 = f32[16,32,128]{2,1,0:T(8,128)S(1)} all-to-all(f32[16,32,128]{2,1,0:T(8,128)S(1)} %broadcast_in_dim.16), channel_id=1, replica_groups=mesh['z'=8,'c'=2,'y'=8,'x'=4] {'z','c'}, dimensions={0} | all-to-all | bytes 524288 | tf_op jit(solution)/shard_map/all_to_all | solution.py:127
  115.1 4.4 %multiply_convert_fusion = (bf16[2048,256]{1,0:T(8,128)(2,1)}, bf16[2048,256]{1,0:T(8,128)(2,1)}) fusion(f32[2048,256]{1,0:T(8,128)} %get-tuple-element.26, f32[2048]{0:T(1024)S(1)} %get-tuple-element.34, f32[256]{0:T(256)S(1)} %dynamic-slice_convert_fusion, f32[2048]{0:T(1024)S(1)} %bitcast.43, f32[2048]{0:T(1024)S(1)} %get-tuple-element.35, ...), kind=kLoop, calls=%fused_computation.9 | loop fusion | flops 5767168 | bytes 5276672 | tf_op jit(solution)/shard_map/convert_element_type | solution.py:172
  119.5 14.9 %shard_map.79 = (f32[8,4,80,256]{3,2,1,0:T(8,128)}, f32[8,112,256]{2,1,0:T(8,128)}, bf16[8,112,256]{2,1,0:T(8,128)(2,1)}, bf16[8,112,256]{2,1,0:T(8,128)(2,1)}, bf16[8,112,256]{2,1,0:T(8,128)(2,1)}) custom-call(bf16[2048,6144]{1,0:T(8,128)(2,1)} %shard_map.77.hot_ref, bf16[2048,256]{1,0:T(8,128)(2,1)} %get-tuple-element.28.grad_ref), custom_call_target="tpu_custom_call" | custom-call | flops 6442450944 | bytes 32505856 | tf_op jit(solution)/shard_map/pallas_call | solution.py:98
  134.3 0.0 copy-start.3
  134.3 0.0 reduce-scatter.2.cloned.1.call-update
  134.3 3.8 %all-to-all-start.3 = ((bf16[16,128,256]{2,1,0:T(8,128)(2,1)}), bf16[16,128,256]{2,1,0:T(8,128)(2,1)S(1)}, u32[]{:S(2)}, u32[]{:S(2)}) async-start(bf16[16,128,256]{2,1,0:T(8,128)(2,1)} %bitcast.38), calls=%async_computation.3 | async-start | bytes 2097152 | tf_op jit(solution)/shard_map/all_to_all | solution.py:183
  138.1 4.0 %collective-permute-start.3 = (bf16[8,112,256]{2,1,0:T(8,128)(2,1)}, bf16[8,112,256]{2,1,0:T(8,128)(2,1)S(1)}, u32[]{:S(2)}, u32[]{:S(2)}) collective-permute-start(bf16[8,112,256]{2,1,0:T(8,128)(2,1)} %get-tuple-element.18), channel_id=1, source_target_pairs={{0,2},{1,3},{2,0},{3,1},{4,6},{5,7},{6,4},{7,5},{8,10},{9,11},{10,... | collective-permute-start | bytes 1376264 | tf_op jit(solution)/shard_map/ppermute | solution.py:180
  142.2 3.7 %collective-permute-start.4 = (bf16[8,112,256]{2,1,0:T(8,128)(2,1)}, bf16[8,112,256]{2,1,0:T(8,128)(2,1)S(1)}, u32[]{:S(2)}, u32[]{:S(2)}) collective-permute-start(bf16[8,112,256]{2,1,0:T(8,128)(2,1)} %get-tuple-element.19), channel_id=1, source_target_pairs={{0,3},{1,0},{2,1},{3,2},{4,7},{5,4},{6,5},{7,6},{8,11},{9,8},{10,9... | collective-permute-start | bytes 1376264 | tf_op jit(solution)/shard_map/ppermute | solution.py:180
  145.8 3.4 %collective-permute-start.5 = (bf16[8,112,256]{2,1,0:T(8,128)(2,1)}, bf16[8,112,256]{2,1,0:T(8,128)(2,1)S(1)}, u32[]{:S(2)}, u32[]{:S(2)}) collective-permute-start(bf16[8,112,256]{2,1,0:T(8,128)(2,1)} %get-tuple-element.20), channel_id=1, source_target_pairs={{0,1},{1,2},{2,3},{3,0},{4,5},{5,6},{6,7},{7,4},{8,9},{9,10},{10,1... | collective-permute-start | bytes 1376264 | tf_op jit(solution)/shard_map/ppermute | solution.py:180
  149.2 6.0 %collective-permute-done.3 = bf16[8,112,256]{2,1,0:T(8,128)(2,1)S(1)} collective-permute-done((bf16[8,112,256]{2,1,0:T(8,128)(2,1)}, bf16[8,112,256]{2,1,0:T(8,128)(2,1)S(1)}, u32[]{:S(2)}, u32[]{:S(2)}) %collective-permute-start.3) | collective-permute-done | bytes 458784 | tf_op jit(solution)/shard_map/ppermute | solution.py:180
  155.2 9.7 %collective-permute-done.4 = bf16[8,112,256]{2,1,0:T(8,128)(2,1)S(1)} collective-permute-done((bf16[8,112,256]{2,1,0:T(8,128)(2,1)}, bf16[8,112,256]{2,1,0:T(8,128)(2,1)S(1)}, u32[]{:S(2)}, u32[]{:S(2)}) %collective-permute-start.4) | collective-permute-done | bytes 458784 | tf_op jit(solution)/shard_map/ppermute | solution.py:180
  164.8 0.4 collective-permute-done.5
  165.2 0.0 copy-done.3
  165.2 1.0 add_convert_fusion
  166.2 0.0 all-to-all-done.3
  166.2 7.3 %all-to-all-start.4 = ((bf16[8,112,256]{2,1,0:T(8,128)(2,1)}), bf16[8,112,256]{2,1,0:T(8,128)(2,1)S(1)}, u32[]{:S(2)}, u32[]{:S(2)}) async-start(bf16[8,112,256]{2,1,0:T(8,128)(2,1)} %add_convert_fusion), calls=%async_computation.5 | async-start | bytes 917504 | tf_op jit(solution)/shard_map/all_to_all | solution.py:189
  173.6 1.1 copy.18
  174.6 6.9 %reduce-scatter.2.cloned.1.call-done = f32[320,256]{1,0:T(8,128)} async-done(((f32[2560,256]{1,0:T(8,128)}), f32[320,256]{1,0:T(8,128)}) %reduce-scatter.2.cloned.1.call-update) | async-done | bytes 327696 | tf_op jit(solution)/shard_map/reduce_scatter | solution.py:177
  181.6 1.0 fusion.10
  182.6 2.8 %collective-permute-start.7 = (f32[80,256]{1,0:T(8,128)S(1)}, f32[80,256]{1,0:T(8,128)S(1)}, u32[]{:S(2)}, u32[]{:S(2)}) collective-permute-start(f32[80,256]{1,0:T(8,128)S(1)} %get-tuple-element.31), channel_id=1, source_target_pairs={{0,2},{1,3},{2,0},{3,1},{4,6},{5,7},{6,4},{7,5},{8,10},{9,11},{10,... | collective-permute-start | bytes 245768 | tf_op jit(solution)/shard_map/ppermute | solution.py:192
  185.4 4.7 %collective-permute-start.8 = (f32[80,256]{1,0:T(8,128)S(1)}, f32[80,256]{1,0:T(8,128)S(1)}, u32[]{:S(2)}, u32[]{:S(2)}) collective-permute-start(f32[80,256]{1,0:T(8,128)S(1)} %get-tuple-element.32), channel_id=1, source_target_pairs={{0,1},{1,2},{2,3},{3,0},{4,5},{5,6},{6,7},{7,4},{8,9},{9,10},{10,1... | collective-permute-start | bytes 245768 | tf_op jit(solution)/shard_map/ppermute | solution.py:192
  190.0 1.9 collective-permute-start.6
  192.0 0.0 all-to-all-done.4
  192.0 0.1 convert_reduce_fusion
  192.0 0.0 collective-permute-done.7
  192.1 0.0 collective-permute-done.8
  192.1 5.5 %collective-permute-done.6 = f32[80,256]{1,0:T(8,128)S(1)} collective-permute-done((f32[80,256]{1,0:T(8,128)S(1)}, f32[80,256]{1,0:T(8,128)S(1)}, u32[]{:S(2)}, u32[]{:S(2)}) %collective-permute-start.6) | collective-permute-done | bytes 81952 | tf_op jit(solution)/shard_map/ppermute | solution.py:192
  197.6 0.9 slice_add_fusion
  198.5 0.7 pad_maximum_fusion.2
  (11 shorter events, 0.2 us)
Async XLA Ops:
  7.2 1.4 copy-start
  7.2 26.6 %copy-start.2 = (bf16[128,4096]{1,0:T(8,128)(2,1)S(1)}, bf16[128,4096]{1,0:T(8,128)(2,1)}, u32[]{:S(2)}) copy-start(bf16[128,4096]{1,0:T(8,128)(2,1)} %param.11) | copy-start | bytes 3145732
  7.2 67.4 %all-gather.2.cloned.1.call-start = ((), (), s32[]{:S(2)}) async-start(), calls=%async_computation.6 | async-start | bytes 3538944 | tf_op jit(solution)/shard_map/all_gather | solution.py:152
  8.6 9.8 %collective-permute-start.2 = (bf16[192,256]{1,0:T(8,128)(2,1)S(1)}, bf16[192,256]{1,0:T(8,128)(2,1)S(1)}, u32[]{:S(2)}, u32[]{:S(2)}) collective-permute-start(bf16[192,256]{1,0:T(8,128)(2,1)S(1)} %constant_dynamic-slice_fusion), channel_id=1, source_target_pairs={{0,3},{1,0},{2,1},{3,2},{4,7},{5,4},{6,5},{7,6},{8,11},{9,8},{10,9... | collective-permute-start | bytes 294920 | tf_op jit(solution)/shard_map/ppermute | solution.py:151
  11.3 8.0 %collective-permute-start.1 = (bf16[192,256]{1,0:T(8,128)(2,1)S(1)}, bf16[192,256]{1,0:T(8,128)(2,1)S(1)}, u32[]{:S(2)}, u32[]{:S(2)}) collective-permute-start(bf16[192,256]{1,0:T(8,128)(2,1)S(1)} %constant_dynamic-slice_fusion), channel_id=1, source_target_pairs={{0,2},{1,3},{2,0},{3,1},{4,6},{5,7},{6,4},{7,5},{8,10},{9,11},{10,... | collective-permute-start | bytes 294920 | tf_op jit(solution)/shard_map/ppermute | solution.py:151
  14.4 6.8 %collective-permute-start = (bf16[192,256]{1,0:T(8,128)(2,1)S(1)}, bf16[192,256]{1,0:T(8,128)(2,1)S(1)}, u32[]{:S(2)}, u32[]{:S(2)}) collective-permute-start(bf16[192,256]{1,0:T(8,128)(2,1)S(1)} %constant_dynamic-slice_fusion), channel_id=1, source_target_pairs={{0,1},{1,2},{2,3},{3,0},{4,5},{5,6},{6,7},{7,4},{8,9},{9,10},{10,1... | collective-permute-start | bytes 294920 | tf_op jit(solution)/shard_map/ppermute | solution.py:151
  23.3 18.1 %all-to-all-start = ((s32[16,4,128]{2,1,0:T(4,128)}), s32[16,4,128]{2,1,0:T(4,128)S(1)}, u32[]{:S(2)}, u32[]{:S(2)}) async-start(s32[16,4,128]{2,1,0:T(4,128)} %broadcast_in_dim.13), calls=%async_computation | async-start | bytes 65536 | tf_op jit(solution)/shard_map/all_to_all | solution.py:127
  41.4 53.6 %all-to-all-start.1 = ((bf16[16,256,256]{2,1,0:T(8,128)(2,1)}), bf16[16,256,256]{2,1,0:T(8,128)(2,1)}, u32[]{:S(2)}, u32[]{:S(2)}) async-start(bf16[16,256,256]{2,1,0:T(8,128)(2,1)} %bitcast.34), calls=%async_computation.1 | async-start | bytes 4194304 | tf_op jit(solution)/shard_map/all_to_all | solution.py:147
  45.9 135.7 %reduce-scatter.2.cloned.1.call-start = ((), (), s32[]{:S(2)}) async-start(), calls=%async_computation.7 | async-start | bytes 2949120 | tf_op jit(solution)/shard_map/reduce_scatter | solution.py:177
  95.1 2.2 %copy-start.1 = (f32[2048,256]{1,0:T(8,128)S(1)}, f32[2048,256]{1,0:T(8,128)}, u32[]{:S(2)}) copy-start(f32[2048,256]{1,0:T(8,128)} %shard_map.78) | copy-start | bytes 6291460
  134.3 30.9 %copy-start.3 = (f32[8,112,256]{2,1,0:T(8,128)S(1)}, f32[8,112,256]{2,1,0:T(8,128)}, u32[]{:S(2)}) copy-start(f32[8,112,256]{2,1,0:T(8,128)} %get-tuple-element.17) | copy-start | bytes 2752516
  134.3 31.9 %all-to-all-start.3 = ((bf16[16,128,256]{2,1,0:T(8,128)(2,1)}), bf16[16,128,256]{2,1,0:T(8,128)(2,1)S(1)}, u32[]{:S(2)}, u32[]{:S(2)}) async-start(bf16[16,128,256]{2,1,0:T(8,128)(2,1)} %bitcast.38), calls=%async_computation.3 | async-start | bytes 2097152 | tf_op jit(solution)/shard_map/all_to_all | solution.py:183
  138.1 17.0 %collective-permute-start.3 = (bf16[8,112,256]{2,1,0:T(8,128)(2,1)}, bf16[8,112,256]{2,1,0:T(8,128)(2,1)S(1)}, u32[]{:S(2)}, u32[]{:S(2)}) collective-permute-start(bf16[8,112,256]{2,1,0:T(8,128)(2,1)} %get-tuple-element.18), channel_id=1, source_target_pairs={{0,2},{1,3},{2,0},{3,1},{4,6},{5,7},{6,4},{7,5},{8,10},{9,11},{10,... | collective-permute-start | bytes 1376264 | tf_op jit(solution)/shard_map/ppermute | solution.py:180
  142.2 22.7 %collective-permute-start.4 = (bf16[8,112,256]{2,1,0:T(8,128)(2,1)}, bf16[8,112,256]{2,1,0:T(8,128)(2,1)S(1)}, u32[]{:S(2)}, u32[]{:S(2)}) collective-permute-start(bf16[8,112,256]{2,1,0:T(8,128)(2,1)} %get-tuple-element.19), channel_id=1, source_target_pairs={{0,3},{1,0},{2,1},{3,2},{4,7},{5,4},{6,5},{7,6},{8,11},{9,8},{10,9... | collective-permute-start | bytes 1376264 | tf_op jit(solution)/shard_map/ppermute | solution.py:180
  145.8 19.4 %collective-permute-start.5 = (bf16[8,112,256]{2,1,0:T(8,128)(2,1)}, bf16[8,112,256]{2,1,0:T(8,128)(2,1)S(1)}, u32[]{:S(2)}, u32[]{:S(2)}) collective-permute-start(bf16[8,112,256]{2,1,0:T(8,128)(2,1)} %get-tuple-element.20), channel_id=1, source_target_pairs={{0,1},{1,2},{2,3},{3,0},{4,5},{5,6},{6,7},{7,4},{8,9},{9,10},{10,1... | collective-permute-start | bytes 1376264 | tf_op jit(solution)/shard_map/ppermute | solution.py:180
  166.2 25.7 %all-to-all-start.4 = ((bf16[8,112,256]{2,1,0:T(8,128)(2,1)}), bf16[8,112,256]{2,1,0:T(8,128)(2,1)S(1)}, u32[]{:S(2)}, u32[]{:S(2)}) async-start(bf16[8,112,256]{2,1,0:T(8,128)(2,1)} %add_convert_fusion), calls=%async_computation.5 | async-start | bytes 917504 | tf_op jit(solution)/shard_map/all_to_all | solution.py:189
  182.6 9.5 %collective-permute-start.7 = (f32[80,256]{1,0:T(8,128)S(1)}, f32[80,256]{1,0:T(8,128)S(1)}, u32[]{:S(2)}, u32[]{:S(2)}) collective-permute-start(f32[80,256]{1,0:T(8,128)S(1)} %get-tuple-element.31), channel_id=1, source_target_pairs={{0,2},{1,3},{2,0},{3,1},{4,6},{5,7},{6,4},{7,5},{8,10},{9,11},{10,... | collective-permute-start | bytes 245768 | tf_op jit(solution)/shard_map/ppermute | solution.py:192
  185.4 6.7 %collective-permute-start.8 = (f32[80,256]{1,0:T(8,128)S(1)}, f32[80,256]{1,0:T(8,128)S(1)}, u32[]{:S(2)}, u32[]{:S(2)}) collective-permute-start(f32[80,256]{1,0:T(8,128)S(1)} %get-tuple-element.32), channel_id=1, source_target_pairs={{0,1},{1,2},{2,3},{3,0},{4,5},{5,6},{6,7},{7,4},{8,9},{9,10},{10,1... | collective-permute-start | bytes 245768 | tf_op jit(solution)/shard_map/ppermute | solution.py:192
  190.0 7.5 %collective-permute-start.6 = (f32[80,256]{1,0:T(8,128)S(1)}, f32[80,256]{1,0:T(8,128)S(1)}, u32[]{:S(2)}, u32[]{:S(2)}) collective-permute-start(f32[80,256]{1,0:T(8,128)S(1)} %get-tuple-element.33), channel_id=1, source_target_pairs={{0,3},{1,0},{2,1},{3,2},{4,7},{5,4},{6,5},{7,6},{8,11},{9,8},{10,9... | collective-permute-start | bytes 245768 | tf_op jit(solution)/shard_map/ppermute | solution.py:192
Sparse Core Ops, SparseCore 0:
  22.1 52.4 all-gather.1
  134.5 47.0 reduce-scatter.1

commit v4 on v3

--- a/solution.py
+++ b/solution.py
@@ -78,7 +78,27 @@
     )(hot, table)
 
 
-def rows_kernel(hot_ref, grad_ref, by_y_ref, *by_x_refs):
+def rows_kernel(
+    hot_ref, hidden_ref, cot_ref, scales_ref, gain_ref, normed_ref, by_y_ref, *rest
+):
+    by_x_refs, grad_ref = rest[:-1], rest[-1]
+    all_tok, width = cot_ref.shape
+    tok = 128
+    blocks = all_tok // tok
+
+    @pl.when(pl.program_id(0) == 0)
+    def _():
+        gain_f = gain_ref[...]
+        for b in range(blocks):
+            here = pl.ds(b * tok, tok)
+            scales = scales_ref[:, here].T
+            inv_rms, pull, count = scales[:, 0:1], scales[:, 1:2], scales[:, 2:3]
+            hidden = hidden_ref[here, :]
+            grad_out = cot_ref[here, :].astype(jnp.float32) * gain_f
+            normed_ref[here, :] = (hidden * inv_rms * gain_f).astype(normed_ref.dtype)
+            grad_hidden = inv_rms * grad_out - hidden * pull
+            grad_ref[here, :] = (grad_hidden / count).astype(grad_ref.dtype)
+
     out = lax.dot_general(
         hot_ref[...],
         grad_ref[...],
@@ -91,31 +111,41 @@
         ref[0] = out[s, ROWS_Y:].astype(ref.dtype)
 
 
-def rows_of(hot, token_grad, rows):
-    tok, width = token_grad.shape
-    span = hot.shape[1]
+def rows_of(hot, hidden, cot, scales, gain_f, rows):
+    width = cot.shape[1]
+    all_tok, span = hot.shape
     late = rows - ROWS_Y
     return pl.pallas_call(
         rows_kernel,
         grid=(Y,),
         in_specs=[
-            pl.BlockSpec((tok, span // Y), lambda i: (0, i)),
-            pl.BlockSpec((tok, width), lambda i: (0, 0)),
-        ],
-        out_specs=[pl.BlockSpec((1, X, ROWS_Y, width), lambda i: (i, 0, 0, 0))]
+            pl.BlockSpec((all_tok, span // Y), lambda i: (0, i)),
+            pl.BlockSpec((all_tok, width), lambda i: (0, 0)),
+            pl.BlockSpec((all_tok, width), lambda i: (0, 0)),
+            pl.BlockSpec(scales.shape, lambda i: (0, 0)),
+            pl.BlockSpec((1, width), lambda i: (0, 0)),
+        ],
+        out_specs=[
+            pl.BlockSpec((all_tok, width), lambda i: (0, 0)),
+            pl.BlockSpec((1, X, ROWS_Y, width), lambda i: (i, 0, 0, 0)),
+        ]
         + [pl.BlockSpec((1, late, width), lambda i: (i, 0, 0))] * X,
-        out_shape=[jax.ShapeDtypeStruct((Y, X, ROWS_Y, width), jnp.float32)]
+        out_shape=[
+            jax.ShapeDtypeStruct((all_tok, width), jnp.bfloat16),
+            jax.ShapeDtypeStruct((Y, X, ROWS_Y, width), jnp.float32),
+        ]
         + [
             jax.ShapeDtypeStruct((Y, late, width), jnp.bfloat16 if s else jnp.float32)
             for s in range(X)
         ],
+        scratch_shapes=[pltpu.VMEM((all_tok, width), jnp.bfloat16)],
         cost_estimate=pl.CostEstimate(
-            flops=2 * tok * width * span,
-            bytes_accessed=2 * tok * (span + width) + 4 * span * width,
+            flops=2 * all_tok * width * span,
+            bytes_accessed=2 * all_tok * (span + 4 * width) + 4 * span * width,
             transcendentals=0,
         ),
         compiler_params=pltpu.CompilerParams(vmem_limit_bytes=60 * 2**20),
-    )(hot, token_grad)
+    )(hot, hidden, cot, scales, gain_f)
 
 
 def shift(s):
@@ -153,36 +183,33 @@
     owner = jnp.arange(Y)[:, None] * X + (here_x - jnp.arange(X)) % X
     table_row = (owner[:, :, None] * rows + jnp.arange(rows)).reshape(all_rows)
 
-    count_f = jnp.sum((ids >= 0).astype(jnp.float32), axis=1, keepdims=True)
     hot = count_matrix(ids, table_row, 256)
 
     gain_f = lax.dynamic_slice(gain, (mine,), (width,)).astype(jnp.float32)
+    gain_f = gain_f.reshape(1, width)
+    count_f = jnp.sum((ids >= 0).astype(jnp.float32), axis=1)
 
     pooled = pool(hot, table, 256)
     pooled, came = lax.optimization_barrier((pooled, came))
     emb = came[:, :tok].reshape(all_tok, width).astype(jnp.float32)
-    cot = came[:, tok:].reshape(all_tok, width).astype(jnp.float32)
-    hidden = emb + pooled / count_f
-    grad_out = cot * gain_f
+    cot = came[:, tok:].reshape(all_tok, width)
+    hidden = emb + pooled / count_f[:, None]
+    grad_out = cot.astype(jnp.float32) * gain_f
     sums = jnp.stack([jnp.sum(hidden * hidden, axis=1), jnp.sum(hidden * grad_out, axis=1)])
     sums = spread(sums.reshape(2 * all_tok // 128, 128), blocks, G)
     sums = jnp.sum(sums.reshape(blocks, 2, all_tok), axis=0) / features
-    inv_rms = lax.rsqrt(sums[0] + 1e-05)[:, None]
-    inner = sums[1][:, None]
-    normed = (hidden * inv_rms * gain_f).astype(jnp.bfloat16)
-    grad_hidden = inv_rms * grad_out - hidden * (inv_rms * inv_rms * inv_rms) * inner
-    token_grad = lax.optimization_barrier((grad_hidden / count_f).astype(jnp.bfloat16))
-
-    by_y, *by_x = rows_of(hot, token_grad, rows)
+    inv_rms = lax.rsqrt(sums[0] + 1e-05)
+    pull = inv_rms * inv_rms * inv_rms * sums[1]
+    scales = jnp.pad(jnp.stack([inv_rms, pull, count_f]), ((0, 5), (0, 0)))
+    normed, by_y, *by_x = rows_of(hot, hidden, cot, scales, gain_f, rows)
+
     by_y = lax.psum_scatter(
         by_y.reshape(Y * X * ROWS_Y, width), "y", scatter_dimension=0, tiled=True
     )
     by_x = [by_x[0]] + [lax.ppermute(by_x[s], "x", shift(-s)) for s in (2, 1, 3)]
     by_x = sum(v.astype(jnp.float32) for v in by_x).astype(jnp.bfloat16)
 
-    back = lax.all_to_all(
-        normed.reshape(blocks, tok, width), G, split_axis=0, concat_axis=0, tiled=True
-    )
+    back = lax.all_to_all(normed.reshape(blocks, tok, width), G, split_axis=0, concat_axis=0, tiled=True)
 
     by_x, back = lax.optimization_barrier((by_x, back))
     normed = back.transpose(1, 0, 2).reshape(tok, features)

time: 207 us -> 207 us (level)
  the two profiles are of different devices: /device:TPU:30 before, /device:TPU:38 now
where the time goes in v4:
time: 207 us; the launch traced here: 206 us
  starting transfers between devices  56.5 us (27%)
  Pallas kernels  50.5 us (24%)
  waiting for transfers between devices  49.3 us (24%)
  blocking collectives  15.7 us (8%)
  between operations  14.3 us (7%)
  local copies, waits for them, and re-layouts  10 us (5%)
  other arithmetic  9.27 us (4%)
    pallas_call x1, Pallas kernels, count_matrix(): pl.pallas_call(functools.partial(count_kernel, step, 256), grid=(rows //...  18.3 us
    pallas_call x1, Pallas kernels, rows_of(): pl.pallas_call(rows_kernel, grid=(Y,), in_specs=[pl.BlockSpec((all_tok, s...  17.2 us
    ppermute x3, waiting for transfers between devices, per_device(): lax.ppermute(by_x[s], 'x', shift(-s))  16 us
    all_to_all x1, blocking collectives, spread(): return lax.all_to_all(whole, axis, split_axis=0, concat_axis=0, tiled=True)  15.7 us
    pallas_call x1, Pallas kernels, pool(): pl.pallas_call(pool_kernel, grid=(tok // block,), in_specs=[pl.BlockSpec(...  15.1 us
    ppermute x3, starting transfers between devices, per_device(): lax.ppermute(by_x[s], 'x', shift(-s))  11.1 us
    all_to_all x1, starting transfers between devices, spread(): return lax.all_to_all(whole, axis, split_axis=0, concat_axis=0, tiled=True)  10.4 us
    ppermute x3, starting transfers between devices, per_device(): pieces = [piece] + [lax.ppermute(piece, 'x', shift(s)) for s in range(1, X)]  9.76 us
  transfers between devices with their start and end apart: 15, of which 10 were waited for; matrix products, arithmetic and copies ran while one was open for 5% of the time, Pallas kernels for 16%

profile of v4, /device:TPU:38, one launch (start us, length us, event | category | flops | bytes accessed | tf_op | source)
XLA Modules:
  0.0 205.5 jit_solution(12171848189182078426)
XLA Ops:
  7.2 0.0 copy-start
  7.2 0.0 copy-start.3
  7.2 0.0 all-gather.2.cloned.1.call-start
  7.2 1.3 copy-done
  8.6 2.7 %collective-permute-start.2 = (bf16[192,256]{1,0:T(8,128)(2,1)S(1)}, bf16[192,256]{1,0:T(8,128)(2,1)S(1)}, u32[]{:S(2)}, u32[]{:S(2)}) collective-permute-start(bf16[192,256]{1,0:T(8,128)(2,1)S(1)} %constant_dynamic-slice_fusion), channel_id=1, source_target_pairs={{0,3},{1,0},{2,1},{3,2},{4,7},{5,4},{6,5},{7,6},{8,11},{9,8},{10,9... | collective-permute-start | bytes 294920 | tf_op jit(solution)/shard_map/ppermute | solution.py:181
  11.3 3.0 %collective-permute-start.1 = (bf16[192,256]{1,0:T(8,128)(2,1)S(1)}, bf16[192,256]{1,0:T(8,128)(2,1)S(1)}, u32[]{:S(2)}, u32[]{:S(2)}) collective-permute-start(bf16[192,256]{1,0:T(8,128)(2,1)S(1)} %constant_dynamic-slice_fusion), channel_id=1, source_target_pairs={{0,2},{1,3},{2,0},{3,1},{4,6},{5,7},{6,4},{7,5},{8,10},{9,11},{10,... | collective-permute-start | bytes 294920 | tf_op jit(solution)/shard_map/ppermute | solution.py:181
  14.4 4.0 %collective-permute-start = (bf16[192,256]{1,0:T(8,128)(2,1)S(1)}, bf16[192,256]{1,0:T(8,128)(2,1)S(1)}, u32[]{:S(2)}, u32[]{:S(2)}) collective-permute-start(bf16[192,256]{1,0:T(8,128)(2,1)S(1)} %constant_dynamic-slice_fusion), channel_id=1, source_target_pairs={{0,1},{1,2},{2,3},{3,0},{4,5},{5,6},{6,7},{7,4},{8,9},{9,10},{10,1... | collective-permute-start | bytes 294920 | tf_op jit(solution)/shard_map/ppermute | solution.py:181
  18.4 0.0 collective-permute-done.2
  18.4 1.0 collective-permute-done.1
  19.4 1.8 collective-permute-done
  21.2 0.8 pad_maximum_fusion.1
  22.0 0.0 all-gather.2.cloned.1.call-update
  22.0 0.7 bitcast_select_fusion
  22.7 0.6 broadcast_in_dim.13
  23.3 10.4 %all-to-all-start = ((s32[16,4,128]{2,1,0:T(4,128)}), s32[16,4,128]{2,1,0:T(4,128)S(1)}, u32[]{:S(2)}, u32[]{:S(2)}) async-start(s32[16,4,128]{2,1,0:T(4,128)} %broadcast_in_dim.13), calls=%async_computation | async-start | bytes 65536 | tf_op jit(solution)/shard_map/all_to_all | solution.py:157
  33.7 0.0 copy-done.3
  33.7 1.4 pad_maximum_fusion
  35.1 1.5 copy.20
  36.7 4.8 %all-to-all-done = s32[16,4,128]{2,1,0:T(4,128)S(1)} async-done(((s32[16,4,128]{2,1,0:T(4,128)}), s32[16,4,128]{2,1,0:T(4,128)S(1)}, u32[]{:S(2)}, u32[]{:S(2)}) %all-to-all-start) | async-done | bytes 32800 | tf_op jit(solution)/shard_map/all_to_all | solution.py:157
  41.4 4.4 %all-to-all-start.1 = ((bf16[16,256,256]{2,1,0:T(8,128)(2,1)}), bf16[16,256,256]{2,1,0:T(8,128)(2,1)}, u32[]{:S(2)}, u32[]{:S(2)}) async-start(bf16[16,256,256]{2,1,0:T(8,128)(2,1)} %bitcast.31), calls=%async_computation.1 | async-start | bytes 4194304 | tf_op jit(solution)/shard_map/all_to_all | solution.py:177
  45.9 0.0 reduce-scatter.2.cloned.1.call-start
  46.0 0.1 add_multiply_fusion
  46.0 0.1 add_convert_fusion.1
  46.1 0.1 convert_element_type.44
  46.2 0.8 dynamic-slice_convert_fusion
  47.0 1.3 copy.15
  48.3 0.8 broadcast_in_dim.14.b_ref
  49.1 18.3 %shard_map.77.hot_ref = bf16[2048,6144]{1,0:T(8,128)(2,1)} custom-call(s32[2048,4]{1,0:T(8,128)} %bitcast.33, s16[32,6144]{1,0:T(8,128)(2,1)} %broadcast_in_dim.14.b_ref), custom_call_target="tpu_custom_call" | custom-call | flops 150994944 | bytes 25165824 | tf_op jit(solution)/shard_map/pallas_call | solution.py:40
  67.4 5.1 %all-gather.2.cloned.1.call-done.table_ref = bf16[6144,256]{1,0:T(8,128)(2,1)} async-done(((bf16[768,256]{1,0:T(8,128)(2,1)}), bf16[6144,256]{1,0:T(8,128)(2,1)}) %all-gather.2.cloned.1.call-update) | async-done | bytes 3145744 | tf_op jit(solution)/shard_map/all_gather | solution.py:182
  72.5 15.1 %shard_map.78 = f32[2048,256]{1,0:T(8,128)} custom-call(bf16[2048,6144]{1,0:T(8,128)(2,1)} %shard_map.77.hot_ref, bf16[6144,256]{1,0:T(8,128)(2,1)} %all-gather.2.cloned.1.call-done.table_ref), custom_call_target="tpu_custom_call" | custom-call | flops 6442450944 | bytes 30408704 | tf_op jit(solution)/shard_map/pallas_call | solution.py:63
  87.6 7.5 %all-to-all-done.1 = bf16[16,256,256]{2,1,0:T(8,128)(2,1)} async-done(((bf16[16,256,256]{2,1,0:T(8,128)(2,1)}), bf16[16,256,256]{2,1,0:T(8,128)(2,1)}, u32[]{:S(2)}, u32[]{:S(2)}) %all-to-all-start.1) | async-done | bytes 2097184 | tf_op jit(solution)/shard_map/all_to_all | solution.py:177
  95.1 1.9 fusion.3
  97.0 0.0 copy-start.1
  97.0 0.0 copy-done.5
  97.0 0.3 copy-done.2
  97.3 2.0 multiply_reduce_fusion.1
  99.3 0.0 copy-done.1
  99.4 15.7 %all_to_all.25 = f32[16,32,128]{2,1,0:T(8,128)S(1)} all-to-all(f32[16,32,128]{2,1,0:T(8,128)S(1)} %broadcast_in_dim.16), channel_id=1, replica_groups=mesh['z'=8,'c'=2,'y'=8,'x'=4] {'z','c'}, dimensions={0} | all-to-all | bytes 524288 | tf_op jit(solution)/shard_map/all_to_all | solution.py:157
  115.1 0.7 select_maximum_fusion.scales_ref
  115.8 17.2 %shard_map.79 = (bf16[2048,256]{1,0:T(8,128)(2,1)}, f32[8,4,80,256]{3,2,1,0:T(8,128)}, f32[8,112,256]{2,1,0:T(8,128)}, bf16[8,112,256]{2,1,0:T(8,128)(2,1)}, bf1...) custom-call(bf16[2048,6144]{1,0:T(8,128)(2,1)} %shard_map.77.hot_ref, f32[2048,256]{1,0:T(8,128)} %get-tuple-element.28.hidden_ref, ...), custom_call_target="tpu_custom_call" | custom-call | flops 6442450944 | bytes 35651584 | tf_op jit(solution)/shard_map/pallas_call | solution.py:118
  133.0 0.0 reduce-scatter.2.cloned.1.call-update
  133.0 3.8 %all-to-all-start.3 = ((bf16[16,128,256]{2,1,0:T(8,128)(2,1)}), bf16[16,128,256]{2,1,0:T(8,128)(2,1)S(1)}, u32[]{:S(2)}, u32[]{:S(2)}) async-start(bf16[16,128,256]{2,1,0:T(8,128)(2,1)} %bitcast.37), calls=%async_computation.3 | async-start | bytes 2097152 | tf_op jit(solution)/shard_map/all_to_all | solution.py:212
  136.8 4.0 %collective-permute-start.3 = (bf16[8,112,256]{2,1,0:T(8,128)(2,1)}, bf16[8,112,256]{2,1,0:T(8,128)(2,1)S(1)}, u32[]{:S(2)}, u32[]{:S(2)}) collective-permute-start(bf16[8,112,256]{2,1,0:T(8,128)(2,1)} %get-tuple-element.19), channel_id=1, source_target_pairs={{0,2},{1,3},{2,0},{3,1},{4,6},{5,7},{6,4},{7,5},{8,10},{9,11},{10,... | collective-permute-start | bytes 1376264 | tf_op jit(solution)/shard_map/ppermute | solution.py:209
  140.8 3.6 %collective-permute-start.4 = (bf16[8,112,256]{2,1,0:T(8,128)(2,1)}, bf16[8,112,256]{2,1,0:T(8,128)(2,1)S(1)}, u32[]{:S(2)}, u32[]{:S(2)}) collective-permute-start(bf16[8,112,256]{2,1,0:T(8,128)(2,1)} %get-tuple-element.20), channel_id=1, source_target_pairs={{0,3},{1,0},{2,1},{3,2},{4,7},{5,4},{6,5},{7,6},{8,11},{9,8},{10,9... | collective-permute-start | bytes 1376264 | tf_op jit(solution)/shard_map/ppermute | solution.py:209
  144.5 3.4 %collective-permute-start.5 = (bf16[8,112,256]{2,1,0:T(8,128)(2,1)}, bf16[8,112,256]{2,1,0:T(8,128)(2,1)S(1)}, u32[]{:S(2)}, u32[]{:S(2)}) collective-permute-start(bf16[8,112,256]{2,1,0:T(8,128)(2,1)} %get-tuple-element.21), channel_id=1, source_target_pairs={{0,1},{1,2},{2,3},{3,0},{4,5},{5,6},{6,7},{7,4},{8,9},{9,10},{10,1... | collective-permute-start | bytes 1376264 | tf_op jit(solution)/shard_map/ppermute | solution.py:209
  147.9 6.0 %collective-permute-done.3 = bf16[8,112,256]{2,1,0:T(8,128)(2,1)S(1)} collective-permute-done((bf16[8,112,256]{2,1,0:T(8,128)(2,1)}, bf16[8,112,256]{2,1,0:T(8,128)(2,1)S(1)}, u32[]{:S(2)}, u32[]{:S(2)}) %collective-permute-start.3) | collective-permute-done | bytes 458784 | tf_op jit(solution)/shard_map/ppermute | solution.py:209
  153.8 9.7 %collective-permute-done.4 = bf16[8,112,256]{2,1,0:T(8,128)(2,1)S(1)} collective-permute-done((bf16[8,112,256]{2,1,0:T(8,128)(2,1)}, bf16[8,112,256]{2,1,0:T(8,128)(2,1)S(1)}, u32[]{:S(2)}, u32[]{:S(2)}) %collective-permute-start.4) | collective-permute-done | bytes 458784 | tf_op jit(solution)/shard_map/ppermute | solution.py:209
  163.5 0.4 collective-permute-done.5
  163.9 1.0 add_convert_fusion
  164.9 0.0 all-to-all-done.3
  164.9 7.2 %all-to-all-start.4 = ((bf16[8,112,256]{2,1,0:T(8,128)(2,1)}), bf16[8,112,256]{2,1,0:T(8,128)(2,1)S(1)}, u32[]{:S(2)}, u32[]{:S(2)}) async-start(bf16[8,112,256]{2,1,0:T(8,128)(2,1)} %add_convert_fusion), calls=%async_computation.5 | async-start | bytes 917504 | tf_op jit(solution)/shard_map/all_to_all | solution.py:216
  172.1 1.1 copy.18
  173.2 7.5 %reduce-scatter.2.cloned.1.call-done = f32[320,256]{1,0:T(8,128)} async-done(((f32[2560,256]{1,0:T(8,128)}), f32[320,256]{1,0:T(8,128)}) %reduce-scatter.2.cloned.1.call-update) | async-done | bytes 327696 | tf_op jit(solution)/shard_map/reduce_scatter | solution.py:206
  180.7 1.0 fusion.4
  181.7 2.8 %collective-permute-start.7 = (f32[80,256]{1,0:T(8,128)S(1)}, f32[80,256]{1,0:T(8,128)S(1)}, u32[]{:S(2)}, u32[]{:S(2)}) collective-permute-start(f32[80,256]{1,0:T(8,128)S(1)} %get-tuple-element.31), channel_id=1, source_target_pairs={{0,2},{1,3},{2,0},{3,1},{4,6},{5,7},{6,4},{7,5},{8,10},{9,11},{10,... | collective-permute-start | bytes 245768 | tf_op jit(solution)/shard_map/ppermute | solution.py:219
  184.5 5.0 %collective-permute-start.8 = (f32[80,256]{1,0:T(8,128)S(1)}, f32[80,256]{1,0:T(8,128)S(1)}, u32[]{:S(2)}, u32[]{:S(2)}) collective-permute-start(f32[80,256]{1,0:T(8,128)S(1)} %get-tuple-element.32), channel_id=1, source_target_pairs={{0,1},{1,2},{2,3},{3,0},{4,5},{5,6},{6,7},{7,4},{8,9},{9,10},{10,1... | collective-permute-start | bytes 245768 | tf_op jit(solution)/shard_map/ppermute | solution.py:219
  189.6 1.9 collective-permute-start.6
  191.5 0.0 all-to-all-done.4
  191.5 0.1 convert_reduce_fusion
  191.6 0.0 collective-permute-done.7
  191.6 0.0 collective-permute-done.8
  191.6 5.5 %collective-permute-done.6 = f32[80,256]{1,0:T(8,128)S(1)} collective-permute-done((f32[80,256]{1,0:T(8,128)S(1)}, f32[80,256]{1,0:T(8,128)S(1)}, u32[]{:S(2)}, u32[]{:S(2)}) %collective-permute-start.6) | collective-permute-done | bytes 81952 | tf_op jit(solution)/shard_map/ppermute | solution.py:219
  197.1 0.9 slice_add_fusion
  198.0 0.7 pad_maximum_fusion.2
  (15 shorter events, 0.2 us)
Async XLA Ops:
  7.2 1.4 copy-start
  7.2 26.6 %copy-start.3 = (bf16[128,4096]{1,0:T(8,128)(2,1)S(1)}, bf16[128,4096]{1,0:T(8,128)(2,1)}, u32[]{:S(2)}) copy-start(bf16[128,4096]{1,0:T(8,128)(2,1)} %param.11) | copy-start | bytes 3145732
  7.2 65.3 %all-gather.2.cloned.1.call-start = ((), (), s32[]{:S(2)}) async-start(), calls=%async_computation.6 | async-start | bytes 3538944 | tf_op jit(solution)/shard_map/all_gather | solution.py:182
  8.6 9.8 %collective-permute-start.2 = (bf16[192,256]{1,0:T(8,128)(2,1)S(1)}, bf16[192,256]{1,0:T(8,128)(2,1)S(1)}, u32[]{:S(2)}, u32[]{:S(2)}) collective-permute-start(bf16[192,256]{1,0:T(8,128)(2,1)S(1)} %constant_dynamic-slice_fusion), channel_id=1, source_target_pairs={{0,3},{1,0},{2,1},{3,2},{4,7},{5,4},{6,5},{7,6},{8,11},{9,8},{10,9... | collective-permute-start | bytes 294920 | tf_op jit(solution)/shard_map/ppermute | solution.py:181
  11.3 8.0 %collective-permute-start.1 = (bf16[192,256]{1,0:T(8,128)(2,1)S(1)}, bf16[192,256]{1,0:T(8,128)(2,1)S(1)}, u32[]{:S(2)}, u32[]{:S(2)}) collective-permute-start(bf16[192,256]{1,0:T(8,128)(2,1)S(1)} %constant_dynamic-slice_fusion), channel_id=1, source_target_pairs={{0,2},{1,3},{2,0},{3,1},{4,6},{5,7},{6,4},{7,5},{8,10},{9,11},{10,... | collective-permute-start | bytes 294920 | tf_op jit(solution)/shard_map/ppermute | solution.py:181
  14.4 6.8 %collective-permute-start = (bf16[192,256]{1,0:T(8,128)(2,1)S(1)}, bf16[192,256]{1,0:T(8,128)(2,1)S(1)}, u32[]{:S(2)}, u32[]{:S(2)}) collective-permute-start(bf16[192,256]{1,0:T(8,128)(2,1)S(1)} %constant_dynamic-slice_fusion), channel_id=1, source_target_pairs={{0,1},{1,2},{2,3},{3,0},{4,5},{5,6},{6,7},{7,4},{8,9},{9,10},{10,1... | collective-permute-start | bytes 294920 | tf_op jit(solution)/shard_map/ppermute | solution.py:181
  23.3 18.1 %all-to-all-start = ((s32[16,4,128]{2,1,0:T(4,128)}), s32[16,4,128]{2,1,0:T(4,128)S(1)}, u32[]{:S(2)}, u32[]{:S(2)}) async-start(s32[16,4,128]{2,1,0:T(4,128)} %broadcast_in_dim.13), calls=%async_computation | async-start | bytes 65536 | tf_op jit(solution)/shard_map/all_to_all | solution.py:157
  41.4 53.7 %all-to-all-start.1 = ((bf16[16,256,256]{2,1,0:T(8,128)(2,1)}), bf16[16,256,256]{2,1,0:T(8,128)(2,1)}, u32[]{:S(2)}, u32[]{:S(2)}) async-start(bf16[16,256,256]{2,1,0:T(8,128)(2,1)} %bitcast.31), calls=%async_computation.1 | async-start | bytes 4194304 | tf_op jit(solution)/shard_map/all_to_all | solution.py:177
  45.9 134.9 %reduce-scatter.2.cloned.1.call-start = ((), (), s32[]{:S(2)}) async-start(), calls=%async_computation.7 | async-start | bytes 2949120 | tf_op jit(solution)/shard_map/reduce_scatter | solution.py:206
  47.0 50.0 %copy-start.5 = (f32[256]{0:T(256)}, f32[256]{0:T(256)S(1)}, u32[]{:S(2)}) copy-start(f32[256]{0:T(256)S(1)} %dynamic-slice_convert_fusion) | copy-start | bytes 3076
  95.1 2.2 %copy-start.2 = (f32[2048,256]{1,0:T(8,128)S(1)}, f32[2048,256]{1,0:T(8,128)}, u32[]{:S(2)}) copy-start(f32[2048,256]{1,0:T(8,128)} %shard_map.78) | copy-start | bytes 6291460
  97.0 2.3 %copy-start.1 = (bf16[16,128,256]{2,1,0:T(8,128)(2,1)}, bf16[16,128,256]{2,1,0:T(8,128)(2,1)S(1)}, u32[]{:S(2)}) copy-start(bf16[16,128,256]{2,1,0:T(8,128)(2,1)S(1)} %get-tuple-element.30) | copy-start | bytes 3145732
  133.0 30.9 %copy-start.4 = (f32[8,112,256]{2,1,0:T(8,128)S(1)}, f32[8,112,256]{2,1,0:T(8,128)}, u32[]{:S(2)}) copy-start(f32[8,112,256]{2,1,0:T(8,128)} %get-tuple-element.18) | copy-start | bytes 2752516
  133.0 31.9 %all-to-all-start.3 = ((bf16[16,128,256]{2,1,0:T(8,128)(2,1)}), bf16[16,128,256]{2,1,0:T(8,128)(2,1)S(1)}, u32[]{:S(2)}, u32[]{:S(2)}) async-start(bf16[16,128,256]{2,1,0:T(8,128)(2,1)} %bitcast.37), calls=%async_computation.3 | async-start | bytes 2097152 | tf_op jit(solution)/shard_map/all_to_all | solution.py:212
  136.8 17.0 %collective-permute-start.3 = (bf16[8,112,256]{2,1,0:T(8,128)(2,1)}, bf16[8,112,256]{2,1,0:T(8,128)(2,1)S(1)}, u32[]{:S(2)}, u32[]{:S(2)}) collective-permute-start(bf16[8,112,256]{2,1,0:T(8,128)(2,1)} %get-tuple-element.19), channel_id=1, source_target_pairs={{0,2},{1,3},{2,0},{3,1},{4,6},{5,7},{6,4},{7,5},{8,10},{9,11},{10,... | collective-permute-start | bytes 1376264 | tf_op jit(solution)/shard_map/ppermute | solution.py:209
  140.8 22.7 %collective-permute-start.4 = (bf16[8,112,256]{2,1,0:T(8,128)(2,1)}, bf16[8,112,256]{2,1,0:T(8,128)(2,1)S(1)}, u32[]{:S(2)}, u32[]{:S(2)}) collective-permute-start(bf16[8,112,256]{2,1,0:T(8,128)(2,1)} %get-tuple-element.20), channel_id=1, source_target_pairs={{0,3},{1,0},{2,1},{3,2},{4,7},{5,4},{6,5},{7,6},{8,11},{9,8},{10,9... | collective-permute-start | bytes 1376264 | tf_op jit(solution)/shard_map/ppermute | solution.py:209
  144.5 19.4 %collective-permute-start.5 = (bf16[8,112,256]{2,1,0:T(8,128)(2,1)}, bf16[8,112,256]{2,1,0:T(8,128)(2,1)S(1)}, u32[]{:S(2)}, u32[]{:S(2)}) collective-permute-start(bf16[8,112,256]{2,1,0:T(8,128)(2,1)} %get-tuple-element.21), channel_id=1, source_target_pairs={{0,1},{1,2},{2,3},{3,0},{4,5},{5,6},{6,7},{7,4},{8,9},{9,10},{10,1... | collective-permute-start | bytes 1376264 | tf_op jit(solution)/shard_map/ppermute | solution.py:209
  164.9 26.6 %all-to-all-start.4 = ((bf16[8,112,256]{2,1,0:T(8,128)(2,1)}), bf16[8,112,256]{2,1,0:T(8,128)(2,1)S(1)}, u32[]{:S(2)}, u32[]{:S(2)}) async-start(bf16[8,112,256]{2,1,0:T(8,128)(2,1)} %add_convert_fusion), calls=%async_computation.5 | async-start | bytes 917504 | tf_op jit(solution)/shard_map/all_to_all | solution.py:216
  181.7 9.9 %collective-permute-start.7 = (f32[80,256]{1,0:T(8,128)S(1)}, f32[80,256]{1,0:T(8,128)S(1)}, u32[]{:S(2)}, u32[]{:S(2)}) collective-permute-start(f32[80,256]{1,0:T(8,128)S(1)} %get-tuple-element.31), channel_id=1, source_target_pairs={{0,2},{1,3},{2,0},{3,1},{4,6},{5,7},{6,4},{7,5},{8,10},{9,11},{10,... | collective-permute-start | bytes 245768 | tf_op jit(solution)/shard_map/ppermute | solution.py:219
  184.5 7.1 %collective-permute-start.8 = (f32[80,256]{1,0:T(8,128)S(1)}, f32[80,256]{1,0:T(8,128)S(1)}, u32[]{:S(2)}, u32[]{:S(2)}) collective-permute-start(f32[80,256]{1,0:T(8,128)S(1)} %get-tuple-element.32), channel_id=1, source_target_pairs={{0,1},{1,2},{2,3},{3,0},{4,5},{5,6},{6,7},{7,4},{8,9},{9,10},{10,1... | collective-permute-start | bytes 245768 | tf_op jit(solution)/shard_map/ppermute | solution.py:219
  189.6 7.5 %collective-permute-start.6 = (f32[80,256]{1,0:T(8,128)S(1)}, f32[80,256]{1,0:T(8,128)S(1)}, u32[]{:S(2)}, u32[]{:S(2)}) collective-permute-start(f32[80,256]{1,0:T(8,128)S(1)} %get-tuple-element.33), channel_id=1, source_target_pairs={{0,3},{1,0},{2,1},{3,2},{4,7},{5,4},{6,5},{7,6},{8,11},{9,8},{10,9... | collective-permute-start | bytes 245768 | tf_op jit(solution)/shard_map/ppermute | solution.py:219
Sparse Core Ops, SparseCore 0:
  22.1 50.3 all-gather.1
  133.1 47.5 reduce-scatter.1
